TPU v7x, 256 devices: a whole 4x4x8 slice. The times are simulated.
256 devices in a mesh: dp: 16 (over x, z_lo, core), tensor: 16 (over y, z_hi).
Axes of the slice: x: 4, y: 4, z: 8 (z_hi: 4, z_lo: 2; z = z_hi * 2 + z_lo), core: 2. Of those that a mesh axis runs over, the one named last changes fastest.
Arguments:
- inputs: bfloat16 [8192, 4096], P(('dp', 'tensor')), may hold values from -60 to 60
- gate_pre: bfloat16 [8192, 7168], P('dp', 'tensor'), may hold values from -6 to 6
- up_pre: bfloat16 [8192, 7168], P('dp', 'tensor'), may hold values from -6 to 6
- grad_out: bfloat16 [8192, 4096], P(('dp', 'tensor')), may hold values from -24 to 24
- gain: float32 [4096], replicated, may hold values from 0.25 to 1.75
- w_gate: bfloat16 [4096, 7168], P(None, 'tensor'), may hold values from -0.09375 to 0.09375
- w_up: bfloat16 [4096, 7168], P(None, 'tensor'), may hold values from -0.09375 to 0.09375
- w_down: bfloat16 [7168, 4096], P('tensor'), may hold values from -0.0625 to 0.0625
Outputs:
- grad_inputs: bfloat16 [8192, 4096], P(('dp', 'tensor'))
- grad_gate: bfloat16 [4096, 7168], P('dp', 'tensor')
- grad_up: bfloat16 [4096, 7168], P('dp', 'tensor')
- grad_down: bfloat16 [7168, 4096], P('tensor', 'dp')
- grad_gain: float32 [4096], replicated
All inputs are finite; a program needn't handle non-finite values.
Results may differ from a plain program's by a relative error of at most 0.023.
Values may be sent and summed in bfloat16 or wider, within the bound.
A program may use at most 128 MiB of HBM per device.

v0:
```python
import jax
import jax.numpy as jnp
from jax import lax
from jax.sharding import PartitionSpec as P


def body(inputs, gate_pre, up_pre, grad_out, gain, w_gate, w_up, w_down):
    wide_inputs = inputs.astype(jnp.float32)
    inv_rms = lax.rsqrt(jnp.mean(wide_inputs * wide_inputs, axis=1, keepdims=True) + 1e-05)
    unit_rows = wide_inputs * inv_rms
    normed = (unit_rows * gain[None, :]).astype(jnp.bfloat16)
    upstream = lax.all_gather(grad_out, "tensor", axis=0, tiled=True)
    gate_wide = gate_pre.astype(jnp.float32)
    up_wide = up_pre.astype(jnp.float32)
    sigmoid_gate = jax.nn.sigmoid(gate_wide)
    hidden = (gate_wide * sigmoid_gate * up_wide).astype(jnp.bfloat16)
    grad_hidden = jnp.dot(upstream, w_down.T, preferred_element_type=jnp.float32)
    grad_gate_pre = (
        grad_hidden * up_wide * sigmoid_gate * (1.0 + gate_wide * (1.0 - sigmoid_gate))
    ).astype(jnp.bfloat16)
    grad_up_pre = (grad_hidden * gate_wide * sigmoid_gate).astype(jnp.bfloat16)
    local_hidden = gate_pre.shape[1]
    piece = lax.all_gather(normed, "tensor", axis=0, tiled=True)
    gate_rows = grad_gate_pre
    up_rows = grad_up_pre
    part_gate = jnp.dot(piece.T, gate_rows, preferred_element_type=jnp.float32)
    part_up = jnp.dot(piece.T, up_rows, preferred_element_type=jnp.float32)
    part_down = jnp.dot(upstream.T, hidden, preferred_element_type=jnp.float32)
    partials = jnp.concatenate([part_gate, part_up, part_down], axis=1)
    summed = lax.psum_scatter(
        partials.astype(jnp.bfloat16), "dp", scatter_dimension=0, tiled=True
    ).astype(jnp.float32)
    grad_gate = summed[:, :local_hidden].astype(jnp.bfloat16)
    grad_up = summed[:, local_hidden : 2 * local_hidden].astype(jnp.bfloat16)
    grad_down = summed[:, 2 * local_hidden :].T.astype(jnp.bfloat16)
    gate_rows = grad_gate_pre
    up_rows = grad_up_pre
    grad_normed = lax.psum_scatter(
        (
            jnp.dot(gate_rows, w_gate.T, preferred_element_type=jnp.float32)
            + jnp.dot(up_rows, w_up.T, preferred_element_type=jnp.float32)
        ).astype(jnp.bfloat16),
        "tensor",
        scatter_dimension=0,
        tiled=True,
    ).astype(jnp.float32)
    grad_gain = lax.psum(jnp.sum(grad_normed * unit_rows, axis=0), ("dp", "tensor"))
    scaled = grad_normed * gain[None, :]
    grad_inputs = (
        grad_out.astype(jnp.float32)
        + inv_rms * (scaled - unit_rows * jnp.mean(scaled * unit_rows, axis=1, keepdims=True))
    ).astype(jnp.bfloat16)
    return (grad_inputs, grad_gate, grad_up, grad_down, grad_gain)


def solution(mesh):
    return jax.shard_map(
        body,
        mesh=mesh,
        in_specs=(
            P(("dp", "tensor"), None),
            P("dp", "tensor"),
            P("dp", "tensor"),
            P(("dp", "tensor"), None),
            P(),
            P(None, "tensor"),
            P(None, "tensor"),
            P("tensor", None),
        ),
        out_specs=(
            P(("dp", "tensor"), None),
            P("dp", "tensor"),
            P("dp", "tensor"),
            P("tensor", "dp"),
            P(),
        ),
        check_vma=False,
    )
```

profile of v0, /device:TPU:1, one launch (start us, length us, event | category | flops | bytes accessed | tf_op | source)
XLA Modules:
  0.0 431.5 jit_solution(17075590688391857334)
XLA Ops:
  7.2 0.0 all-gather.3.cloned.1.call-start
  7.2 0.7 all-gather.3.cloned.1.call-update
  7.9 0.0 reduce-scatter.3.cloned.1.call-start
  7.9 81.0 %all-gather.3.cloned.1.call-done = bf16[512,4096]{1,0:T(8,128)(2,1)} async-done(((bf16[32,4096]{1,0:T(8,128)(2,1)}), bf16[512,4096]{1,0:T(8,128)(2,1)}) %all-gather.3.cloned.1.call-update) | async-done | bytes 4194320 | tf_op jit(solution)/shard_map/all_gather | solution.py:12
  89.0 0.0 copy-start
  89.0 5.9 %fusion.3 = (bf16[512,448]{0,1:T(8,128)(2,1)S(1)}, f32[512,448]{0,1:T(8,128)S(1)}) fusion(bf16[512,448]{0,1:T(8,128)(2,1)} %param.10, bf16[512,448]{0,1:T(8,128)(2,1)} %param.9, bf16[512,4096]{1,0:T(8,128)(2,1)} %all-gather.3.cloned.1.call-done, bf16[448,4096]{1,0:T(8,128)(2,1)} %param.15), kind=kOutput, calls=%fused_computation.14 | convolution fusion | flops 1881800704 | bytes 10158080 | tf_op jit(solution)/shard_map/dot_general | solution.py:17
  94.9 0.0 copy-done
  94.9 0.0 copy-start.7
  94.9 0.0 copy-start.9
  94.9 2.4 fusion.27
  97.3 0.0 copy-done.7
  97.3 0.0 copy-done.9
  97.3 4.7 %add_convert_fusion = bf16[512,4096]{1,0:T(8,128)(2,1)} fusion(f32[512,4096]{1,0:T(8,128)S(1)} %fusion.27, bf16[4096,448]{0,1:T(8,128)(2,1)S(1)} %copy-done.7, f32[512,448]{0,1:T(8,128)S(1)} %get-tuple-element.12, bf16[512,448]{0,1:T(8,128)(2,1)S(1)} %copy-done.9), kind=kOutput, calls=%fused_computation.1 | convolution fusion | flops 1884848128 | bytes 17629184 | tf_op jit(solution)/shard_map/dot_general | solution.py:41
  102.0 0.0 copy-start.2
  102.0 0.0 copy-start.5
  102.0 0.0 copy-start.8
  102.0 0.0 reduce-scatter.3.cloned.1.call-update
  102.1 0.0 all-gather.5.cloned.1.call-start
  102.1 0.9 copy-done.2
  103.0 0.2 fusion.20
  103.2 95.2 %reduce-scatter.3.cloned.1.call-done = bf16[32,4096]{1,0:T(8,128)(2,1)} async-done(((bf16[512,4096]{1,0:T(8,128)(2,1)}), bf16[32,4096]{1,0:T(8,128)(2,1)}) %reduce-scatter.3.cloned.1.call-update) | async-done | bytes 262160 | tf_op jit(solution)/shard_map/reduce_scatter | solution.py:38
  198.4 0.0 copy-done.5
  198.4 2.0 fusion.21
  200.4 0.0 all-gather.5.cloned.1.call-update
  200.4 0.2 reduce-scatter.5.cloned.1.call-start
  200.6 0.0 copy-done.8
  200.6 6.2 %fusion = bf16[4096,448]{0,1:T(8,128)(2,1)} fusion(bf16[512,4096]{1,0:T(8,128)(2,1)} %all-gather.3.cloned.1.call-done, bf16[512,448]{0,1:T(8,128)(2,1)S(1)} %copy-done.8, bf16[512,448]{0,1:T(8,128)(2,1)S(1)} %copy-done.9), kind=kOutput, calls=%fused_computation.5 | convolution fusion | flops 1882718208 | bytes 8781824 | tf_op jit(solution)/shard_map/dot_general | solution.py:28
  206.8 68.0 %all-gather.5.cloned.1.call-done = bf16[512,4096]{1,0:T(8,128)(2,1)} async-done(((bf16[32,4096]{1,0:T(8,128)(2,1)}), bf16[512,4096]{1,0:T(8,128)(2,1)}) %all-gather.5.cloned.1.call-update) | async-done | bytes 4194320 | tf_op jit(solution)/shard_map/all_gather | solution.py:23
  274.8 0.0 copy-start.6
  274.8 4.5 %convolution_convert_fusion = bf16[4096,448]{0,1:T(8,128)(2,1)S(1)} fusion(bf16[512,4096]{1,0:T(8,128)(2,1)} %all-gather.5.cloned.1.call-done, f32[512,448]{0,1:T(8,128)S(1)} %get-tuple-element.12, bf16[512,448]{0,1:T(8,128)(2,1)S(1)} %copy-done.9), kind=kOutput, calls=%fused_computation.2 | convolution fusion | flops 1882488832 | bytes 9240576 | tf_op jit(solution)/shard_map/dot_general | solution.py:27
  279.3 0.0 copy-done.6
  279.3 0.0 copy-start.1
  279.3 2.1 convolution_convert_fusion.1
  281.4 0.0 copy-done.1
  281.4 14.1 %pad_maximum_fusion = bf16[4096,1344]{0,1:T(8,128)(2,1)} fusion(bf16[4096,448]{0,1:T(8,128)(2,1)S(1)} %copy-done.1, bf16[4096,448]{0,1:T(8,128)(2,1)S(1)} %convolution_convert_fusion, bf16[4096,448]{0,1:T(8,128)(2,1)S(1)} %convolution_convert_fusion.1), kind=kLoop, calls=%fused_computation | loop fusion | flops 33030144 | bytes 22020096 | tf_op jit(solution)/shard_map/concatenate | solution.py:29
  295.5 0.0 copy-start.3
  295.5 0.0 copy-start.4
  295.5 0.0 reduce-scatter.5.cloned.1.call-update
  295.6 80.4 %psum.7 = f32[4096]{0:T(1024)} all-reduce(f32[4096]{0:T(1024)S(1)} %get-tuple-element.5), channel_id=1, replica_groups=mesh['dp'=16,'tensor'=16] {'dp','tensor'}, use_global_device_ids=true, to_apply=%region_5.0 | all-reduce | flops 4096 | bytes 32768 | tf_op jit(solution)/shard_map/psum | solution.py:47
  375.9 0.0 copy-done.3
  375.9 0.0 copy-done.4
  375.9 0.9 fusion.17
  376.8 46.1 %reduce-scatter.5.cloned.1.call-done = bf16[256,1344]{0,1:T(8,128)(2,1)} async-done(((bf16[4096,1344]{0,1:T(8,128)(2,1)}), bf16[256,1344]{0,1:T(8,128)(2,1)}) %reduce-scatter.5.cloned.1.call-update) | async-done | bytes 688144 | tf_op jit(solution)/shard_map/reduce_scatter | solution.py:30
  423.0 2.0 slice_bitcast_fusion
  (2 shorter events, 0.0 us)
Async XLA Ops:
  7.2 81.8 %all-gather.3.cloned.1.call-start = ((), (), s32[]{:S(2)}) async-start(), calls=%async_computation.2 | async-start | bytes 4456448 | tf_op jit(solution)/shard_map/all_gather | solution.py:12
  7.9 190.5 %reduce-scatter.3.cloned.1.call-start = ((), (), s32[]{:S(2)}) async-start(), calls=%async_computation.3 | async-start | bytes 4456448 | tf_op jit(solution)/shard_map/reduce_scatter | solution.py:38
  89.0 5.9 %copy-start = (bf16[4096,448]{0,1:T(8,128)(2,1)S(1)}, bf16[4096,448]{0,1:T(8,128)(2,1)}, u32[]{:S(2)}) copy-start(bf16[4096,448]{0,1:T(8,128)(2,1)} %param.13) | copy-start | bytes 11010052
  94.9 2.4 copy-start.7
  94.9 2.4 copy-start.9
  102.0 0.9 copy-start.2
  102.0 96.3 %copy-start.5 = (f32[4096]{0:T(1024)S(1)}, f32[4096]{0:T(1024)}, u32[]{:S(2)}) copy-start(f32[4096]{0:T(1024)} %param.12) | copy-start | bytes 49156
  102.0 98.6 %copy-start.8 = (bf16[512,448]{0,1:T(8,128)(2,1)S(1)}, bf16[512,448]{0,1:T(8,128)(2,1)}, u32[]{:S(2)}) copy-start(bf16[512,448]{0,1:T(8,128)(2,1)} %param.10) | copy-start | bytes 1376260
  102.1 172.8 %all-gather.5.cloned.1.call-start = ((), (), s32[]{:S(2)}) async-start(), calls=%async_computation.4 | async-start | bytes 4456448 | tf_op jit(solution)/shard_map/all_gather | solution.py:23
  200.4 222.6 %reduce-scatter.5.cloned.1.call-start = ((), (), s32[]{:S(2)}) async-start(), calls=%async_computation.5 | async-start | bytes 11698176 | tf_op jit(solution)/shard_map/reduce_scatter | solution.py:30
  274.8 4.5 %copy-start.6 = (bf16[512,4096]{1,0:T(8,128)(2,1)S(1)}, bf16[512,4096]{1,0:T(8,128)(2,1)}, u32[]{:S(2)}) copy-start(bf16[512,4096]{1,0:T(8,128)(2,1)} %all-gather.5.cloned.1.call-done) | copy-start | bytes 12582916
  279.3 2.1 copy-start.1
  295.5 80.4 %copy-start.3 = (bf16[32,4096]{1,0:T(8,128)(2,1)S(1)}, bf16[32,4096]{1,0:T(8,128)(2,1)}, u32[]{:S(2)}) copy-start(bf16[32,4096]{1,0:T(8,128)(2,1)} %param.11) | copy-start | bytes 786436
  295.5 80.4 %copy-start.4 = (bf16[32,4096]{1,0:T(8,128)(2,1)S(1)}, bf16[32,4096]{1,0:T(8,128)(2,1)}, u32[]{:S(2)}) copy-start(bf16[32,4096]{1,0:T(8,128)(2,1)} %reduce-scatter.3.cloned.1.call-done) | copy-start | bytes 786436
Sparse Core Ops, SparseCore 0:
  10.4 78.4 all-gather.2
  102.2 96.1 reduce-scatter.2
  201.7 73.0 all-gather.4
  295.7 127.2 reduce-scatter.4
where the time goes:
time: 432 us
  waiting for transfers between devices  291 us (67%)
  blocking collectives  80.4 us (19%)
  matrix products  25.7 us (6%)
  other arithmetic  17.2 us (4%)
  between operations  13.9 us (3%)
    reduce_scatter x1, waiting for transfers between devices, body(): lax.psum_scatter((jnp.dot(gate_rows, w_gate.T, preferred_element_type=jnp...  95.2 us
    all_gather x1, waiting for transfers between devices, body(): upstream = lax.all_gather(grad_out, 'tensor', axis=0, tiled=True)  81 us
    psum x1, blocking collectives, body(): lax.psum(jnp.sum(grad_normed * unit_rows, axis=0), ('dp', 'tensor'))  80.4 us
    all_gather x1, waiting for transfers between devices, body(): piece = lax.all_gather(normed, 'tensor', axis=0, tiled=True)  68 us
    reduce_scatter x1, waiting for transfers between devices, body(): lax.psum_scatter(partials.astype(jnp.bfloat16), 'dp', scatter_dimension=0...  46.1 us
    concatenate x1, other arithmetic, body(): partials = jnp.concatenate([part_gate, part_up, part_down], axis=1)  14.1 us
  transfers between devices with their start and end apart: 4, of which 4 were waited for; matrix products, arithmetic and copies ran while one was open for 2% of the time, Pallas kernels for 0%

commit v1 on v0

v1 whole, which is shorter than its diff:
```python
import functools

import jax
import jax.numpy as jnp
from jax import lax
from jax.experimental import pallas as pl
from jax.experimental.pallas import tpu as pltpu
from jax.sharding import PartitionSpec as P

MESH = pl.DeviceIdType.MESH
BF = jnp.bfloat16
F32 = jnp.float32
D = 4096
F = 448
T = 512
NQ = 4
QW = D // NQ
KS = (0, 1, 3, 2)
RELS = (2, 1, 3, 0)


def dot_nt(a, b):
    return lax.dot_general(a, b, (((1,), (1,)), ((), ())), preferred_element_type=F32)


def dot_nn(a, b):
    return lax.dot_general(a, b, (((1,), (0,)), ((), ())), preferred_element_type=F32)


def kernel(
    inputs, gate_pre, up_pre, grad_out, gain, w_gate, w_up, w_down,
    o_in, o_gate, o_up, o_down, o_gain,
    vin, vgain, vgp, vup, wg, wu, wd,
    g_all, g_sib, n_all, n_send, a1, a2, gh, acts, act_t, act_s,
    part, rh, rf, rs, zh_buf, zf_buf, gn,
    xp_d, xh_d, xf_d, xz_d, xp_w, xh_w, xf_w, xz_w,
    gy, gz, og,
    loc, ag_s, ag_r, r_s, r_r, x_s, x_r, c_s, c_r, g_s, g_r,
):
    p = lax.axis_index("dp")
    t = lax.axis_index("tensor")
    x, zl, c = p // 4, lax.rem(p // 2, 2), lax.rem(p, 2)
    y, zh = t // 4, lax.rem(t, 4)
    oc = 1 - c
    sib = (x * 4 + zl * 2 + oc, t)
    zsib = (x * 4 + (1 - zl) * 2 + c, t)

    def ring(v, k):
        return lax.rem(v + k, 4)

    def ydev(k):
        return (p, ring(y, k) * 4 + zh)

    def zdev(k):
        return (p, y * 4 + ring(zh, k))

    def xdev(k):
        return (ring(x, k) * 4 + zl * 2 + c, t)

    def tid(ky, kz):
        return ring(y, ky) * 4 + ring(zh, kz)

    sent = []

    def send(src, dst, ss, rs_, dev):
        cp = pltpu.make_async_remote_copy(
            src_ref=src, dst_ref=dst, send_sem=ss, recv_sem=rs_, device_id=dev, device_id_type=MESH
        )
        cp.start()
        sent.append(cp)

    def recv(dst, sem, ss, dev):
        pltpu.make_async_remote_copy(
            src_ref=dst, dst_ref=dst, send_sem=ss, recv_sem=sem, device_id=dev, device_id_type=MESH
        ).wait_recv()

    local = []
    for i, (src, dst) in enumerate((
        (inputs, vin), (gain, vgain), (gate_pre, vgp), (up_pre, vup),
        (grad_out, g_all.at[t]), (w_down, wd), (w_gate, wg), (w_up, wu),
    )):
        cp = pltpu.make_async_copy(src, dst, loc.at[i])
        cp.start()
        local.append(cp)

    barrier = pltpu.get_barrier_semaphore()
    partners = [ydev(k) for k in (1, 2, 3)] + [zdev(k) for k in (1, 2, 3)] + [xdev(k) for k in (1, 2, 3)] + [sib, zsib]
    for dev in partners:
        pl.semaphore_signal(barrier, inc=1, device_id=dev, device_id_type=MESH)
    pl.semaphore_wait(barrier, len(partners))

    class Gather:
        def __init__(self, item, q, zfirst, piece, half, own):
            self.piece_t, self.half_t, self.own = piece, half, own
            self.zfirst = zfirst
            self.s = lambda i: ag_s.at[item, q, i]
            self.r = lambda i: ag_r.at[item, q, i]
            self.dev1 = zdev if zfirst else ydev
            self.dev2 = ydev if zfirst else zdev

        def tt(self, ku, kv):
            return tid(kv, ku) if self.zfirst else tid(ku, kv)

        def piece(self, ku, kv):
            return self.piece_t(self.tt(ku, kv))

        def half(self, ku, kv, h):
            return self.half_t(self.tt(ku, kv), h)

        def push(self, src, dst, i, dev):
            send(src, dst, self.s(i), self.r(i), dev)

        def second(self, k, src=None):
            i = KS.index(k)
            ref = self.piece(k, 0)
            src = ref if src is None else src
            self.push(src, ref, 4 + 2 * i + 1, self.dev2(1))
            self.push(src, ref, 4 + 2 * i, self.dev2(3))

        def e0(self):
            ref = self.piece(0, 0)
            src = ref if self.own is None else self.own
            self.push(src, ref, 1, self.dev1(1))
            self.push(src, ref, 0, self.dev1(3))
            self.second(0, src)

        def e1(self):
            recv(self.piece(1, 0), self.r(0), self.s(0), self.dev1(1))
            self.push(self.half(1, 0, 0), self.half(1, 0, 0), 2, self.dev1(3))
            self.second(1)
            recv(self.piece(3, 0), self.r(1), self.s(1), self.dev1(3))
            self.push(self.half(3, 0, 1), self.half(3, 0, 1), 3, self.dev1(1))
            self.second(3)

        def fwd(self, k):
            i = KS.index(k)
            recv(self.piece(k, 1), self.r(4 + 2 * i), self.s(4 + 2 * i), self.dev2(1))
            self.push(self.half(k, 1, 0), self.half(k, 1, 0), 12 + 2 * i, self.dev2(3))
            recv(self.piece(k, 3), self.r(4 + 2 * i + 1), self.s(4 + 2 * i + 1), self.dev2(3))
            self.push(self.half(k, 3, 1), self.half(k, 3, 1), 12 + 2 * i + 1, self.dev2(1))

        def e3(self):
            recv(self.half(2, 0, 0), self.r(2), self.s(2), self.dev1(1))
            recv(self.half(2, 0, 1), self.r(3), self.s(3), self.dev1(3))
            self.second(2)

        def e7(self):
            for i, k in enumerate(KS):
                recv(self.half(k, 2, 0), self.r(12 + 2 * i), self.s(12 + 2 * i), self.dev2(1))
                recv(self.half(k, 2, 1), self.r(12 + 2 * i + 1), self.s(12 + 2 * i + 1), self.dev2(3))

    def g_cols(q):
        return pl.ds(q * QW, QW)

    def n_cols(q):
        return pl.ds(pl.multiple_of(ring(x, RELS[q]) * 512, 512), 512)

    GA = [
        Gather(
            0, q, True,
            lambda tt, q=q: g_all.at[tt, :, g_cols(q)],
            lambda tt, h, q=q: g_all.at[tt, pl.ds(16 * h, 16), g_cols(q)],
            grad_out.at[:, g_cols(q)],
        )
        for q in range(NQ)
    ]
    NA = [
        Gather(
            1, q, True,
            lambda tt, q=q: n_all.at[:, tt, :, n_cols(q)],
            lambda tt, h, q=q: n_all.at[h, tt, :, n_cols(q)],
            None,
        )
        for q in range(NQ)
    ]

    for q in range(NQ):
        GA[q].e0()

    local[0].wait()
    local[1].wait()
    xin = vin[...].astype(F32)
    inv = lax.rsqrt(jnp.mean(xin * xin, axis=1, keepdims=True) + 1e-05)

    @pl.loop(0, 8)
    def _(j):
        own = pl.ds(pl.multiple_of((2 * j + c) * 256, 256), 256)
        oth = pl.ds(pl.multiple_of((2 * j + oc) * 256, 256), 256)
        col = pl.ds(pl.multiple_of(j * 256, 256), 256)
        n_all[c, t, :, col] = (vin[:, own].astype(F32) * inv * vgain[:, own]).astype(BF)
        n_send[:, col] = (vin[:, oth].astype(F32) * inv * vgain[:, oth]).astype(BF)

    send(n_send, n_all.at[c, t], c_s.at[0], c_r.at[0], sib)

    local[2].wait()
    local[3].wait()

    @pl.loop(0, 4)
    def _(r):
        rows = pl.ds(pl.multiple_of(r * 128, 128), 128)
        gp = vgp[rows, :].astype(F32)
        up = vup[rows, :].astype(F32)
        s = jax.nn.sigmoid(gp)
        gs = gp * s
        a2[rows, :] = gs
        a1[rows, :] = up * (s * (1.0 + gp * (1.0 - s)))
        act_t[0, :, rows] = (gs * up).T.astype(BF)

    send(act_t.at[0], act_s.at[0], c_s.at[1], c_r.at[1], sib)

    for q in range(NQ):
        GA[q].e1()
        GA[q].fwd(0)
    for q in range(NQ):
        GA[q].e3()
        GA[q].fwd(1)
        GA[q].fwd(3)
    recv(n_all.at[oc, t], c_r.at[0], c_s.at[0], sib)
    local[4].wait()
    local[5].wait()
    for q in range(NQ):
        GA[q].fwd(2)
        if q >= 1:
            NA[q - 1].e0()
        GA[q].e7()
        v = dot_nt(g_all[:, :, g_cols(q)].reshape(T, QW), wd[:, g_cols(q)])
        if q == 0:
            gh[...] = v
        else:
            gh[...] += v
        for jj in range(2):
            j = 2 * q + jj
            src = g_all.at[:, :, pl.ds(pl.multiple_of((2 * j + oc) * 256, 256), 256)]
            send(src, g_sib.at[:, :, pl.ds(j * 256, 256)], c_s.at[4 + j], c_r.at[4 + j], sib)
    NA[3].e0()

    @pl.loop(0, 4)
    def _(r):
        rows = pl.ds(pl.multiple_of(r * 128, 128), 128)
        v = gh[rows, :]
        vg = v * a1[rows, :]
        vu = v * a2[rows, :]
        acts[0, rows, :] = vg.astype(BF)
        acts[1, rows, :] = vu.astype(BF)
        act_t[1, :, rows] = vg.T.astype(BF)
        act_t[2, :, rows] = vu.T.astype(BF)

    for i in (1, 2):
        send(act_t.at[i], act_s.at[i], c_s.at[1 + i], c_r.at[1 + i], sib)

    for q in range(NQ):
        NA[q].e1()
        NA[q].fwd(0)

    def add_rows(dst, srcs, rows, step):
        @pl.loop(0, rows // step)
        def _(r):
            rr = pl.ds(pl.multiple_of(r * step, step), step)
            v = dst[rr, :].astype(F32)
            for s_ in srcs:
                v = v + s_[rr, :].astype(F32)
            dst[rr, :] = v.astype(BF)

    class XSum:
        def __init__(self, base, rows, xp, xh, xf, xz):
            self.rows, self.xp, self.xh, self.xf, self.xz = rows, xp, xh, xf, xz
            self.s = lambda i: x_s.at[base + i]
            self.r = lambda i: x_r.at[base + i]

        def push(self, src, dst, i, dev):
            send(src, dst, self.s(i), self.r(i), dev)

        def step(self, rel):
            xr = ring(x, rel)
            if rel == 2:
                self.push(self.xp.at[xr, 0], self.xh.at[0], 0, xdev(1))
                self.push(self.xp.at[xr, 1], self.xh.at[1], 1, xdev(3))
            elif rel == 1:
                recv(self.xh.at[0], self.r(0), self.s(0), xdev(3))
                add_rows(self.xp.at[xr, 0], [self.xh.at[0]], self.rows, 64)
                self.push(self.xp.at[xr], self.xf.at[0], 2, xdev(1))
            elif rel == 3:
                recv(self.xh.at[1], self.r(1), self.s(1), xdev(1))
                add_rows(self.xp.at[xr, 1], [self.xh.at[1]], self.rows, 64)
                self.push(self.xp.at[xr], self.xf.at[1], 3, xdev(3))

        def cross(self):
            recv(self.xf.at[0], self.r(2), self.s(2), xdev(3))
            recv(self.xf.at[1], self.r(3), self.s(3), xdev(1))
            oz = 1 - zl
            add_rows(self.xp.at[x, oz], [self.xf.at[0, oz], self.xf.at[1, oz]], self.rows, 64)
            self.push(self.xp.at[x, oz], self.xz, 4, zsib)

        def total(self, rr):
            v = self.xp[x, zl, rr, :].astype(F32) + self.xf[0, zl, rr, :].astype(F32)
            return v + self.xf[1, zl, rr, :].astype(F32) + self.xz[rr, :].astype(F32)

        def arrive(self):
            recv(self.xz, self.r(4), self.s(4), zsib)

    XD = XSum(0, F, xp_d, xh_d, xf_d, xz_d)
    XW = XSum(5, 2 * F, xp_w, xh_w, xf_w, xz_w)

    def down_part(rel):
        xr = ring(x, rel)

        @pl.loop(0, 2)
        def _(z):
            j = xr * 2 + z
            mine = g_all[:, :, pl.ds(pl.multiple_of((2 * j + c) * 256, 256), 256)].reshape(T, 256)
            his = g_sib[:, :, pl.ds(pl.multiple_of(j * 256, 256), 256)].reshape(T, 256)
            xp_d[xr, z] = (dot_nn(act_t[0], mine) + dot_nn(act_s[0], his)).astype(BF)

    def weight_part(rel):
        xr = ring(x, rel)

        @pl.loop(0, 4)
        def _(i):
            z, k = i // 2, lax.rem(i, 2)
            cols = pl.ds(pl.multiple_of((xr * 2 + z) * 256, 256), 256)
            mine = n_all[c, :, :, cols].reshape(T, 256)
            his = n_all[oc, :, :, cols].reshape(T, 256)
            v = dot_nn(act_t[1 + k], mine) + dot_nn(act_s[1 + k], his)
            xp_w[xr, z, pl.ds(pl.multiple_of(k * F, F), F), :] = v.astype(BF)

    def p_part(i):
        cols = pl.ds(i * 512, 512)
        v = dot_nt(acts[0], wg[cols, :]) + dot_nt(acts[1], wu[cols, :])
        part[:, :, cols] = v.astype(BF).reshape(16, 32, 512)

    recv(act_s.at[0], c_r.at[1], c_s.at[1], sib)
    for j in range(8):
        recv(g_sib.at[:, :, pl.ds(j * 256, 256)], c_r.at[4 + j], c_s.at[4 + j], sib)
    local[6].wait()
    local[7].wait()
    for q in range(NQ):
        down_part(RELS[q])
        NA[q].e3()
        NA[q].fwd(1)
        NA[q].fwd(3)
        XD.step(RELS[q])
        p_part(2 * q)
        p_part(2 * q + 1)

    class Scatter:
        def __init__(self, q):
            self.cols = pl.ds(q * QW, QW)
            self.s = lambda i: r_s.at[q, i]
            self.r = lambda i: r_r.at[q, i]

        def push(self, src, dst, i, dev):
            send(src, dst, self.s(i), self.r(i), dev)

        def blk(self, ky, kz):
            return part.at[tid(ky, kz), :, self.cols]

        def hblk(self, ky, kz, h):
            return part.at[tid(ky, kz), pl.ds(16 * h, 16), self.cols]

        def r0(self, k):
            i = KS.index(k)
            self.push(self.hblk(2, k, 0), rh.at[i, 0, :, self.cols], 2 * i, ydev(1))
            self.push(self.hblk(2, k, 1), rh.at[i, 1, :, self.cols], 2 * i + 1, ydev(3))

        def r1(self, k):
            i = KS.index(k)
            for h, ky in ((0, 1), (1, 3)):
                src = rh.at[i, h, :, self.cols]
                recv(src, self.r(2 * i + h), self.s(2 * i + h), ydev(4 - ky))
                dst = self.hblk(ky, k, h)
                dst[...] = (dst[...].astype(F32) + src[...].astype(F32)).astype(BF)
                self.push(self.blk(ky, k), rf.at[i, h, :, self.cols], 8 + 2 * i + h, ydev(ky))

        def r2(self, k):
            i = KS.index(k)
            for h, ky in ((0, 3), (1, 1)):
                recv(rf.at[i, h, :, self.cols], self.r(8 + 2 * i + h), self.s(8 + 2 * i + h), ydev(ky))
            v = self.blk(0, k)[...].astype(F32) + rf[i, 0, :, self.cols].astype(F32)
            v = v + rf[i, 1, :, self.cols].astype(F32)
            rs[i, :, self.cols] = v.astype(BF)
            if k == 2:
                for h, kz in ((0, 1), (1, 3)):
                    src = rs.at[i, pl.ds(16 * h, 16), self.cols]
                    self.push(src, zh_buf.at[h, :, self.cols], 16 + h, zdev(kz))

        def r4(self):
            for h, kz in ((0, 1), (1, 3)):
                src = zh_buf.at[h, :, self.cols]
                recv(src, self.r(16 + h), self.s(16 + h), zdev(4 - kz))
                i = KS.index(kz)
                dst = rs.at[i, pl.ds(16 * h, 16), self.cols]
                dst[...] = (dst[...].astype(F32) + src[...].astype(F32)).astype(BF)
                self.push(rs.at[i, :, self.cols], zf_buf.at[h, :, self.cols], 18 + h, zdev(kz))

        def r5(self):
            for h, kz in ((0, 3), (1, 1)):
                recv(zf_buf.at[h, :, self.cols], self.r(18 + h), self.s(18 + h), zdev(kz))
            v = rs[0, :, self.cols].astype(F32) + zf_buf[0, :, self.cols].astype(F32)
            gn[:, self.cols] = v + zf_buf[1, :, self.cols].astype(F32)

    RA = [Scatter(q) for q in range(NQ)]
    ORDER = (2, 1, 3, 0)

    for i in (1, 2):
        recv(act_s.at[i], c_r.at[1 + i], c_s.at[1 + i], sib)
    for q in range(NQ):
        NA[q].fwd(2)
        if q >= 2:
            for k in ORDER:
                RA[q - 2].r0(k)
        NA[q].e7()
        weight_part(RELS[q])
        XW.step(RELS[q])
        if q == 0:
            XD.cross()
    XD.arrive()

    @pl.loop(0, F // 64)
    def _(r):
        rr = pl.ds(pl.multiple_of(r * 64, 64), 64)
        o_down[rr, :] = XD.total(rr).astype(BF)

    for q in range(NQ):
        for k in ORDER:
            RA[q].r1(k)
        if q + 2 < NQ:
            for k in ORDER:
                RA[q + 2].r0(k)
        if q >= 1:
            RA[q - 1].r4()
        for k in ORDER:
            RA[q].r2(k)
        if q == 1:
            XW.cross()

    XW.arrive()
    blk = pl.ds(pl.multiple_of(p * 256, 256), 256)
    gsum = jnp.zeros((1, 256), F32)
    for k, (o_ref, w_ref) in enumerate(((o_gate, wg), (o_up, wu))):
        v = XW.total(pl.ds(k * F, F))
        gsum = gsum + jnp.sum(v * w_ref[blk, :].astype(F32).T, axis=0, keepdims=True)
        o_ref[...] = v.T.astype(BF)
    gsum = gsum / vgain[:, blk]
    gy[y] = jnp.broadcast_to(gsum, (8, 256))
    for k in (1, 2, 3):
        send(gy.at[y], gy.at[y], g_s.at[k], g_r.at[k], ydev(k))

    RA[NQ - 1].r4()

    for k in (1, 2, 3):
        yk = ring(y, 4 - k)
        recv(gy.at[yk], g_r.at[k], g_s.at[k], ydev(4 - k))
    gz[zh] = gy[0] + gy[1] + gy[2] + gy[3]
    for k in (1, 2, 3):
        send(gz.at[zh], gz.at[zh], g_s.at[3 + k], g_r.at[3 + k], zdev(k))
    for q in range(NQ - 1):
        RA[q].r5()
    for k in (1, 2, 3):
        zk = ring(zh, 4 - k)
        recv(gz.at[zk], g_r.at[3 + k], g_s.at[3 + k], zdev(4 - k))
    og[p] = gz[0] + gz[1] + gz[2] + gz[3]
    send(og.at[p], og.at[p], g_s.at[7], g_r.at[7], sib)
    psib = x * 4 + zl * 2 + oc
    recv(og.at[psib], g_r.at[7], g_s.at[7], sib)
    pair = x * 4 + zl * 2
    opair = x * 4 + (1 - zl) * 2
    send(og.at[pl.ds(pair, 2)], og.at[pl.ds(pair, 2)], g_s.at[8], g_r.at[8], zsib)
    recv(og.at[pl.ds(opair, 2)], g_r.at[8], g_s.at[8], zsib)
    for k in (1, 2, 3):
        send(og.at[pl.ds(x * 4, 4)], og.at[pl.ds(x * 4, 4)], g_s.at[8 + k], g_r.at[8 + k], xdev(k))

    RA[NQ - 1].r5()
    xin = vin[...].astype(F32)
    inv = lax.rsqrt(jnp.mean(xin * xin, axis=1, keepdims=True) + 1e-05)
    dotp = jnp.zeros((32, 1), F32)
    for q in range(NQ):
        cols = pl.ds(q * QW, QW)
        dotp = dotp + jnp.sum(gn[:, cols] * vgain[:, cols] * (vin[:, cols].astype(F32) * inv), axis=1, keepdims=True)
    dotp = dotp * (1.0 / D)
    for q in range(NQ):
        cols = pl.ds(q * QW, QW)
        unit = vin[:, cols].astype(F32) * inv
        res = g_all[t, :, cols].astype(F32) + inv * (gn[:, cols] * vgain[:, cols] - unit * dotp)
        o_in[:, cols] = res.astype(BF)

    for k in (1, 2, 3):
        xk = ring(x, 4 - k)
        recv(og.at[pl.ds(xk * 4, 4)], g_r.at[8 + k], g_s.at[8 + k], xdev(4 - k))
    o_gain[...] = og[:, 0, :]
    for cp in sent:
        cp.wait_send()


def body(inputs, gate_pre, up_pre, grad_out, gain, w_gate, w_up, w_down):
    V = pltpu.VMEM
    DMA = pltpu.SemaphoreType.DMA
    any_spec = pl.BlockSpec(memory_space=pl.ANY)
    vm_spec = pl.BlockSpec(memory_space=pltpu.VMEM)
    outs = pl.pallas_call(
        kernel,
        out_shape=(
            jax.ShapeDtypeStruct((32, D), BF),
            jax.ShapeDtypeStruct((256, F), BF),
            jax.ShapeDtypeStruct((256, F), BF),
            jax.ShapeDtypeStruct((F, 256), BF),
            jax.ShapeDtypeStruct((16, 256), F32),
        ),
        in_specs=[any_spec] * 8,
        out_specs=(vm_spec,) * 5,
        scratch_shapes=[
            V((32, D), BF), V((1, D), F32), V((T, F), BF), V((T, F), BF),
            V((D, F), BF), V((D, F), BF), V((F, D), BF),
            V((16, 32, D), BF), V((16, 32, D // 2), BF), V((2, 16, 32, D // 2), BF), V((32, D // 2), BF),
            V((T, F), F32), V((T, F), F32), V((T, F), F32),
            V((2, T, F), BF), V((3, F, T), BF), V((3, F, T), BF),
            V((16, 32, D), BF), V((4, 2, 16, D), BF), V((4, 2, 32, D), BF), V((4, 32, D), BF),
            V((2, 16, D), BF), V((2, 32, D), BF), V((32, D), F32),
            V((4, 2, F, 256), BF), V((2, F, 256), BF), V((2, 2, F, 256), BF), V((F, 256), BF),
            V((4, 2, 2 * F, 256), BF), V((2, 2 * F, 256), BF), V((2, 2, 2 * F, 256), BF), V((2 * F, 256), BF),
            V((4, 8, 256), F32), V((4, 8, 256), F32), V((16, 8, 256), F32),
            DMA((8,)), DMA((2, NQ, 20)), DMA((2, NQ, 20)), DMA((NQ, 20)), DMA((NQ, 20)),
            DMA((10,)), DMA((10,)), DMA((12,)), DMA((12,)), DMA((12,)), DMA((12,)),
        ],
        compiler_params=pltpu.CompilerParams(
            collective_id=0, has_side_effects=True, vmem_limit_bytes=60 * 2**20
        ),
    )(inputs, gate_pre, up_pre, grad_out, gain.reshape(1, D), w_gate, w_up, w_down)
    return outs[0], outs[1], outs[2], outs[3], outs[4].reshape(D)


def solution(mesh):
    return jax.shard_map(
        body,
        mesh=mesh,
        in_specs=(
            P(("dp", "tensor"), None),
            P("dp", "tensor"),
            P("dp", "tensor"),
            P(("dp", "tensor"), None),
            P(),
            P(None, "tensor"),
            P(None, "tensor"),
            P("tensor", None),
        ),
        out_specs=(
            P(("dp", "tensor"), None),
            P("dp", "tensor"),
            P("dp", "tensor"),
            P("tensor", "dp"),
            P(),
        ),
        check_vma=False,
    )
```

time: 432 us -> 188 us (0.44)
  waiting for transfers between devices: 291 us -> 0 us
  Pallas kernels: 0 us -> 161 us
  blocking collectives: 80.4 us -> 0 us
  matrix products: 25.7 us -> 0 us
  local copies, waits for them, and re-layouts: 2.92 us -> 25.2 us
  other arithmetic: 17.2 us -> 0 us
  between operations: 13.9 us -> 0.64 us
    pallas_call x0 -> x1, Pallas kernels: none -> 161 us  [body(): pl.pallas_call(kernel, out_shape=(jax.ShapeDtypeStruct((32, D), BF), jax....]
    all_gather x2 -> x0, waiting for transfers between devices: 149 us -> none  [the longest x1 81 us: body(): upstream = lax.all_gather(grad_out, 'tensor', axis=0, tiled=True)]
    reduce_scatter x2 -> x0, waiting for transfers between devices: 141 us -> none  [the longest x1 95.2 us: body(): lax.psum_scatter((jnp.dot(gate_rows, w_gate.T, preferred_element_type=jnp...]
    psum x1 -> x0, blocking collectives: 80.4 us -> none  [body(): lax.psum(jnp.sum(grad_normed * unit_rows, axis=0), ('dp', 'tensor'))]
    dot_general x6 -> x0, matrix products: 25.7 us -> none  [the longest x1 6.18 us: body(): part_down = jnp.dot(upstream.T, hidden, preferred_element_type=jnp.float32)]
    unnamed x20 -> x9, local copies, waits for them, and re-layouts: 0.91 us -> 25.2 us
    concatenate x1 -> x0, other arithmetic: 14.1 us -> none  [body(): partials = jnp.concatenate([part_gate, part_up, part_down], axis=1)]
  transfers between devices with their start and end apart: 4 -> 0, of which waited for: 4 -> 0; matrix products, arithmetic and copies ran while one was open for 2% -> 0% of each run, Pallas kernels for 0% -> 0%
where the time goes in v1:
time: 188 us; the launch traced here: 187 us
  Pallas kernels  161 us (86%)
  local copies, waits for them, and re-layouts  25.2 us (13%)
    pallas_call x1, Pallas kernels, body(): pl.pallas_call(kernel, out_shape=(jax.ShapeDtypeStruct((32, D), BF), jax....  161 us
    unnamed x9, local copies, waits for them, and re-layouts  25.2 us

profile of v1, /device:TPU:1, one launch (start us, length us, event | category | flops | bytes accessed | tf_op | source)
XLA Modules:
  0.0 187.3 jit_solution(11596625040550659186)
XLA Ops:
  0.6 2.1 %copy.13.gate_pre = bf16[512,448]{1,0:T(8,128)(2,1)} copy(bf16[512,448]{0,1:T(8,128)(2,1)} %param.9) | data formatting | bytes 917504 | tf_op args[1]
  2.7 2.1 %copy.14.up_pre = bf16[512,448]{1,0:T(8,128)(2,1)} copy(bf16[512,448]{0,1:T(8,128)(2,1)} %param.10) | data formatting | bytes 917504 | tf_op args[2]
  4.8 6.4 %copy.15.w_gate = bf16[4096,448]{1,0:T(8,128)(2,1)} copy(bf16[4096,448]{0,1:T(8,128)(2,1)} %param.13) | data formatting | bytes 7340032 | tf_op args[5]
  11.2 6.5 %copy.16.w_up = bf16[4096,448]{1,0:T(8,128)(2,1)} copy(bf16[4096,448]{0,1:T(8,128)(2,1)} %param.14) | data formatting | bytes 7340032 | tf_op args[6]
  17.7 161.5 %shard_map.119 = (bf16[32,4096]{1,0:T(8,128)(2,1)}, bf16[256,448]{1,0:T(8,128)(2,1)}, bf16[256,448]{1,0:T(8,128)(2,1)}, bf16[448,256]{1,0:T(8,128)(2,1)}, f32[16,256]{1,0:T(8,128)}) custom-call(bf16[32,4096]{1,0:T(8,128)(2,1)} %inputs.1, bf16[512,448]{1,0:T(8,128)(2,1)} %copy.13.gate_pre, bf16[512,448]{1,0:T(8,128)(2,1)} %copy.14.up_pre, ...), custom_call_target="tpu_custom_call" | custom-call | tf_op jit(solution)/shard_map/pallas_call | solution.py:499
  179.1 1.3 copy.19
  180.5 1.8 copy.17
  182.2 1.8 copy.18
  184.0 1.7 copy.22
  185.7 1.6 copy.23

commit v2 on v0

v2 whole, which is shorter than its diff:
```python
import functools

import jax
import jax.numpy as jnp
from jax import lax
from jax.experimental import pallas as pl
from jax.experimental.pallas import tpu as pltpu
from jax.sharding import PartitionSpec as P

MESH = pl.DeviceIdType.MESH
BF = jnp.bfloat16
F32 = jnp.float32
D = 4096
F = 448
T = 512
NQ = 4
QW = D // NQ
KS = (0, 1, 3, 2)
MODES = {'G': 'zzzy', 'N': 'zzzz', 'R': 'zzzy'}
ORDER = (
    ('G', 'e0', 2), ('normed',), ('G', 'e0', 0), ('G', 's2', 0, 0), ('G', 'e0', 1), ('G', 'e0', 3), ('G', 's2', 3, 0),
    ('G', 's2', 1, 0), ('prefac',), ('nx',), ('G', 's2', 2, 0), ('G', 'f2', 0, 0, 3), ('G', 'f2', 0, 0, 1),
    ('G', 'f1', 2, 3), ('G', 'f1', 2, 1), ('G', 's2', 2, 3), ('G', 'f1', 3, 3), ('G', 'f1', 3, 1), ('G', 's2', 3, 3),
    ('G', 's2', 3, 1), ('G', 's2', 2, 1), ('G', 'f2', 1, 0, 3), ('G', 'f2', 1, 0, 1), ('G', 'f1', 0, 3),
    ('G', 's2', 0, 3), ('G', 'f1', 0, 1), ('G', 's2', 0, 1), ('G', 'f2', 2, 0, 3), ('G', 'f2', 2, 0, 1),
    ('G', 'f2', 2, 3, 3), ('G', 'f2', 2, 3, 1), ('G', 'f1', 1, 3), ('G', 'f1', 1, 1), ('G', 's2', 1, 3),
    ('G', 's2', 1, 1), ('G', 'e3', 3), ('G', 's2', 3, 2), ('G', 'f2', 2, 1, 3), ('G', 'f2', 2, 1, 1),
    ('G', 'f2', 3, 0, 3), ('G', 'f2', 3, 0, 1), ('G', 'f2', 0, 3, 3), ('G', 'f2', 0, 3, 1), ('G', 'e3', 2),
    ('G', 's2', 2, 2), ('G', 'f2', 0, 1, 3), ('G', 'f2', 0, 1, 1), ('G', 'f2', 3, 3, 3), ('G', 'f2', 3, 3, 1),
    ('G', 'f2', 1, 3, 3), ('G', 'f2', 1, 3, 1), ('G', 'f2', 1, 1, 3), ('G', 'f2', 1, 1, 1), ('G', 'f2', 3, 1, 3),
    ('G', 'f2', 3, 1, 1), ('G', 'e3', 0), ('G', 's2', 0, 2), ('G', 'f2', 2, 2, 3), ('G', 'f2', 2, 2, 1),
    ('G', 'e3', 1), ('G', 's2', 1, 2), ('G', 'f2', 3, 2, 3), ('G', 'f2', 3, 2, 1), ('G', 'f2', 0, 2, 3),
    ('G', 'f2', 0, 2, 1), ('G', 'done', 2), ('gh', 2), ('G', 'f2', 1, 2, 3), ('G', 'f2', 1, 2, 1), ('N', 'e0', 0),
    ('N', 's2', 0, 0), ('G', 'done', 0), ('gh', 0), ('G', 'done', 3), ('N', 'e0', 1), ('N', 's2', 1, 0),
    ('G', 'done', 1), ('gh', 1), ('N', 'f2', 0, 0, 3), ('N', 'f2', 0, 0, 1), ('gh', 3), ('acts',),
    ('N', 'f2', 1, 0, 3), ('N', 'f2', 1, 0, 1), ('N', 'f1', 0, 3), ('N', 'f1', 0, 1), ('N', 's2', 0, 3),
    ('N', 's2', 0, 1), ('dready',), ('D', 'part', 2), ('D', 'x2'), ('N', 'e0', 2), ('N', 's2', 2, 0),
    ('D', 'part', 1), ('D', 'part', 3), ('D', 'part', 0), ('wready',), ('N', 'f1', 1, 3), ('N', 's2', 1, 3),
    ('N', 'e3', 0), ('N', 's2', 0, 2), ('N', 'f1', 1, 1), ('N', 'f2', 0, 3, 3), ('N', 'f2', 0, 3, 1), ('tr',),
    ('pp', 5), ('N', 'f2', 0, 1, 3), ('N', 'f2', 0, 1, 1), ('N', 'f1', 2, 3), ('N', 'f1', 2, 1), ('N', 's2', 1, 1),
    ('pp', 6), ('N', 'f2', 2, 0, 3), ('N', 'f2', 2, 0, 1), ('N', 'e0', 3), ('N', 'e3', 1), ('N', 's2', 1, 2),
    ('N', 'f2', 1, 3, 3), ('N', 'f2', 1, 3, 1), ('D', 'x1'), ('D', 'x3'), ('pp', 4), ('N', 'f2', 0, 2, 3),
    ('N', 'f2', 0, 2, 1), ('pp', 2), ('N', 'e3', 2), ('N', 's2', 2, 3), ('pp', 1), ('N', 'f2', 1, 1, 3),
    ('N', 'f2', 1, 1, 1), ('pp', 0), ('N', 's2', 2, 1), ('N', 'f1', 3, 3), ('N', 'f1', 3, 1), ('pp', 3),
    ('N', 'f2', 1, 2, 3), ('N', 'f2', 1, 2, 1), ('N', 's2', 2, 2), ('pp', 7), ('N', 'done', 0), ('W', 'part', 2),
    ('N', 'e3', 3), ('N', 'f2', 2, 3, 3), ('N', 'f2', 2, 3, 1), ('N', 's2', 3, 0), ('W', 'x2'), ('R', 'r0', 3, 2),
    ('N', 's2', 3, 3), ('R', 'r0', 3, 1), ('R', 'r0', 3, 3), ('R', 'r0', 3, 0), ('N', 'f2', 2, 1, 3),
    ('N', 'f2', 2, 1, 1), ('N', 'done', 1), ('W', 'part', 1), ('N', 'f2', 2, 2, 3), ('N', 'f2', 2, 2, 1),
    ('N', 's2', 3, 1), ('W', 'x1i'), ('D', 'cross'), ('N', 's2', 3, 2), ('R', 'r1', 3, 2, 0), ('R', 'r1', 3, 2, 1),
    ('N', 'f2', 3, 0, 3), ('N', 'f2', 3, 0, 1), ('R', 'r1', 3, 1, 0), ('R', 'r1', 3, 1, 1), ('N', 'f2', 3, 3, 3),
    ('N', 'f2', 3, 3, 1), ('R', 'r1', 3, 3, 0), ('R', 'r1', 3, 3, 1), ('R', 'r0', 0, 2), ('N', 'done', 2),
    ('W', 'part', 3), ('W', 'x3i'), ('N', 'f2', 3, 1, 3), ('N', 'f2', 3, 1, 1), ('R', 'r1', 3, 0, 0),
    ('R', 'r1', 3, 0, 1), ('R', 'r0', 0, 1), ('N', 'f2', 3, 2, 3), ('N', 'f2', 3, 2, 1), ('R', 'r0', 0, 3),
    ('R', 'r0', 0, 0), ('R', 'r0', 1, 2), ('R', 'r1', 0, 2, 0), ('R', 'r1', 0, 2, 1), ('W', 'x1d'), ('W', 'x3d'),
    ('D', 'fin'), ('N', 'done', 3), ('W', 'part', 0), ('R', 'r1', 1, 2, 0), ('R', 'r1', 1, 2, 1),
    ('R', 'r1', 0, 1, 0), ('R', 'r1', 0, 1, 1), ('R', 'r1', 0, 3, 0), ('R', 'r1', 0, 3, 1), ('R', 'r2', 0, 2),
    ('R', 'r1', 0, 0, 0), ('R', 'r1', 0, 0, 1), ('R', 'r2', 3, 2), ('R', 'r2', 3, 1), ('R', 'r2', 1, 2),
    ('R', 'r2', 3, 3), ('R', 'r0', 2, 2), ('R', 'r0', 1, 1), ('R', 'r2', 0, 1), ('R', 'r0', 2, 1), ('R', 'r0', 1, 3),
    ('R', 'r2', 0, 3), ('R', 'r2', 3, 0), ('R', 'r0', 2, 3), ('R', 'r0', 1, 0), ('R', 'r4', 0, 0), ('R', 'r4', 0, 1),
    ('R', 'r4', 3, 0), ('R', 'r4', 3, 1), ('R', 'r2', 0, 0), ('R', 'r1', 2, 2, 0), ('R', 'r1', 2, 2, 1),
    ('R', 'r1', 1, 1, 0), ('R', 'r1', 1, 1, 1), ('R', 'r1', 2, 1, 0), ('R', 'r1', 2, 1, 1), ('W', 'cross'),
    ('R', 'r1', 1, 3, 0), ('R', 'r1', 1, 3, 1), ('R', 'r1', 2, 3, 0), ('R', 'r1', 1, 0, 0), ('R', 'r1', 1, 0, 1),
    ('R', 'r1', 2, 3, 1), ('R', 'r5', 0), ('R', 'r5', 3), ('R', 'r2', 2, 2), ('R', 'r2', 1, 1), ('R', 'r4', 1, 0),
    ('R', 'r0', 2, 0), ('R', 'r2', 2, 1), ('R', 'r2', 1, 3), ('R', 'r4', 1, 1), ('R', 'r2', 1, 0), ('R', 'r2', 2, 3),
    ('R', 'r1', 2, 0, 0), ('R', 'r1', 2, 0, 1), ('W', 'fin'), ('R', 'r4', 2, 0), ('R', 'r4', 2, 1), ('R', 'r2', 2, 0),
    ('R', 'r5', 1), ('gain1',), ('R', 'r5', 2), ('fin',), ('gain2',),
)
RELS = (2, 1, 3, 0)


def dot_nt(a, b):
    return lax.dot_general(a, b, (((1,), (1,)), ((), ())), preferred_element_type=F32)


def dot_nn(a, b):
    return lax.dot_general(a, b, (((1,), (0,)), ((), ())), preferred_element_type=F32)


def kernel(
    inputs, gate_pre, up_pre, grad_out, gain, w_gate, w_up, w_down,
    o_in, o_gate, o_up, o_down, o_gain,
    vin, vgain, vgp, vup, wg, wu, wd,
    g_all, g_sib, n_all, n_send, a1, a2, gh, acts, act_t, act_s,
    part, rh, rf, rs, zh_buf, zf_buf, gn,
    xp_d, xh_d, xf_d, xz_d, xp_w, xh_w, xf_w, xz_w,
    gt, og,
    loc, ag_s, ag_r, r_s, r_r, x_s, x_r, c_s, c_r, g_s, g_r,
):
    p = lax.axis_index("dp")
    t = lax.axis_index("tensor")
    x, zl, c = p // 4, lax.rem(p // 2, 2), lax.rem(p, 2)
    y, zh = t // 4, lax.rem(t, 4)
    oc = 1 - c
    sib = (x * 4 + zl * 2 + oc, t)
    zsib = (x * 4 + (1 - zl) * 2 + c, t)

    def ring(v, k):
        return lax.rem(v + k, 4)

    def ydev(k):
        return (p, ring(y, k) * 4 + zh)

    def zdev(k):
        return (p, y * 4 + ring(zh, k))

    def xdev(k):
        return (ring(x, k) * 4 + zl * 2 + c, t)

    def tdev(k):
        return (p, lax.rem(t + k, 16))

    def pdev(k):
        return (lax.rem(p + k, 16), t)

    def tid(ky, kz):
        return ring(y, ky) * 4 + ring(zh, kz)

    sent = []

    def send(src, dst, ss, rs_, dev):
        cp = pltpu.make_async_remote_copy(
            src_ref=src, dst_ref=dst, send_sem=ss, recv_sem=rs_, device_id=dev, device_id_type=MESH
        )
        cp.start()
        sent.append(cp)

    def recv(dst, sem, ss, dev):
        pltpu.make_async_remote_copy(
            src_ref=dst, dst_ref=dst, send_sem=ss, recv_sem=sem, device_id=dev, device_id_type=MESH
        ).wait_recv()

    barrier = pltpu.get_barrier_semaphore()
    partners = [f(k) for f in (ydev, zdev, xdev) for k in (1, 3)] + [sib, zsib]
    for dev in partners:
        pl.semaphore_signal(barrier, inc=1, device_id=dev, device_id_type=MESH)
    local = []
    for i, (src, dst) in enumerate((
        (inputs, vin), (gain, vgain), (gate_pre, vgp), (up_pre, vup),
        (grad_out, g_all.at[t]), (w_down, wd), (w_gate, wg), (w_up, wu),
    )):
        cp = pltpu.make_async_copy(src, dst, loc.at[i])
        cp.start()
        local.append(cp)

    local[0].wait()
    local[1].wait()
    xin = vin[...].astype(F32)
    inv = lax.rsqrt(jnp.mean(xin * xin, axis=1, keepdims=True) + 1e-05)

    @pl.loop(0, 8)
    def _(j):
        own = pl.ds(pl.multiple_of((2 * j + c) * 256, 256), 256)
        oth = pl.ds(pl.multiple_of((2 * j + oc) * 256, 256), 256)
        col = pl.ds(pl.multiple_of(j * 256, 256), 256)
        n_all[c, t, :, col] = (vin[:, own].astype(F32) * inv * vgain[:, own]).astype(BF)
        n_send[:, col] = (vin[:, oth].astype(F32) * inv * vgain[:, oth]).astype(BF)
    pl.semaphore_wait(barrier, len(partners))

    class Gather:
        def __init__(self, item, q, zfirst, piece, half, own):
            self.piece_t, self.half_t, self.own = piece, half, own
            self.zfirst = zfirst
            self.s = lambda i: ag_s.at[item, q, i]
            self.r = lambda i: ag_r.at[item, q, i]
            self.dev1 = zdev if zfirst else ydev
            self.dev2 = ydev if zfirst else zdev

        def tt(self, ku, kv):
            return tid(kv, ku) if self.zfirst else tid(ku, kv)

        def piece(self, ku, kv):
            return self.piece_t(self.tt(ku, kv))

        def half(self, ku, kv, h):
            return self.half_t(self.tt(ku, kv), h)

        def push(self, src, dst, i, dev):
            send(src, dst, self.s(i), self.r(i), dev)

        def e0(self):
            ref = self.piece(0, 0)
            src = ref if self.own is None else self.own
            self.push(src, ref, 1, self.dev1(1))
            self.push(src, ref, 0, self.dev1(3))

        def s2(self, k):
            i = KS.index(k)
            ref = self.piece(k, 0)
            src = ref if self.own is None or k else self.own
            self.push(src, ref, 4 + 2 * i + 1, self.dev2(1))
            self.push(src, ref, 4 + 2 * i, self.dev2(3))

        def f1(self, k):
            h = k // 2
            recv(self.piece(k, 0), self.r(h), self.s(h), self.dev1(k))
            self.push(self.half(k, 0, h), self.half(k, 0, h), 2 + h, self.dev1(4 - k))

        def f2(self, k, kk):
            i, h = KS.index(k), kk // 2
            recv(self.piece(k, kk), self.r(4 + 2 * i + h), self.s(4 + 2 * i + h), self.dev2(kk))
            self.push(self.half(k, kk, h), self.half(k, kk, h), 12 + 2 * i + h, self.dev2(4 - kk))

        def e3(self):
            recv(self.half(2, 0, 0), self.r(2), self.s(2), self.dev1(1))
            recv(self.half(2, 0, 1), self.r(3), self.s(3), self.dev1(3))

        def done(self):
            for i, k in enumerate(KS):
                recv(self.half(k, 2, 0), self.r(12 + 2 * i), self.s(12 + 2 * i), self.dev2(1))
                recv(self.half(k, 2, 1), self.r(12 + 2 * i + 1), self.s(12 + 2 * i + 1), self.dev2(3))

    def g_cols(q):
        return pl.ds(q * QW, QW)

    def n_cols(q):
        return pl.ds(pl.multiple_of(ring(x, RELS[q]) * 512, 512), 512)

    GA = [
        Gather(
            0, q, MODES['G'][q] == 'z',
            lambda tt, q=q: g_all.at[tt, :, g_cols(q)],
            lambda tt, h, q=q: g_all.at[tt, pl.ds(16 * h, 16), g_cols(q)],
            grad_out.at[:, g_cols(q)],
        )
        for q in range(NQ)
    ]
    NA = [
        Gather(
            1, q, MODES['N'][q] == 'z',
            lambda tt, q=q: n_all.at[:, tt, :, n_cols(q)],
            lambda tt, h, q=q: n_all.at[h, tt, :, n_cols(q)],
            None,
        )
        for q in range(NQ)
    ]

    def normed():
        send(n_send, n_all.at[c, t], c_s.at[0], c_r.at[0], sib)

    def nx():
        recv(n_all.at[oc, t], c_r.at[0], c_s.at[0], sib)

    def prefac():
        local[2].wait()
        local[3].wait()

        @pl.loop(0, F // 64)
        def _(r):
            rows = pl.ds(pl.multiple_of(r * 64, 64), 64)
            gp = vgp[rows, :].astype(F32)
            up = vup[rows, :].astype(F32)
            s = jax.nn.sigmoid(gp)
            gs = gp * s
            a2[rows, :] = gs
            a1[rows, :] = up * (s * (1.0 + gp * (1.0 - s)))
            act_t[0, rows, :] = (gs * up).astype(BF)

        send(act_t.at[0], act_s.at[0], c_s.at[1], c_r.at[1], sib)

    begun = set()

    def gh_add(q):
        if "gh" not in begun:
            local[4].wait()
            local[5].wait()
        v = dot_nt(wd[:, g_cols(q)], g_all[:, :, g_cols(q)].reshape(T, QW))
        gh[...] = v if "gh" not in begun else gh[...] + v
        begun.add("gh")
        for jj in range(2):
            j = 2 * q + jj
            src = g_all.at[:, :, pl.ds(pl.multiple_of((2 * j + oc) * 256, 256), 256)]
            send(src, g_sib.at[:, :, pl.ds(j * 256, 256)], c_s.at[4 + j], c_r.at[4 + j], sib)

    def act_grads():
        @pl.loop(0, F // 64)
        def _(r):
            rows = pl.ds(pl.multiple_of(r * 64, 64), 64)
            v = gh[rows, :]
            act_t[1, rows, :] = (v * a1[rows, :]).astype(BF)
            act_t[2, rows, :] = (v * a2[rows, :]).astype(BF)

        for i in (1, 2):
            send(act_t.at[i], act_s.at[i], c_s.at[1 + i], c_r.at[1 + i], sib)

    def turn():
        @pl.loop(0, 4)
        def _(r):
            rows = pl.ds(pl.multiple_of(r * 128, 128), 128)
            for i in (1, 2):
                acts[i - 1, rows, :] = act_t[i, :, rows].T

    def d_ready():
        recv(act_s.at[0], c_r.at[1], c_s.at[1], sib)
        for j in range(8):
            recv(g_sib.at[:, :, pl.ds(j * 256, 256)], c_r.at[4 + j], c_s.at[4 + j], sib)

    def w_ready():
        for i in (1, 2):
            recv(act_s.at[i], c_r.at[1 + i], c_s.at[1 + i], sib)

    def add_rows(dst, srcs, rows, step):
        @pl.loop(0, rows // step)
        def _(r):
            rr = pl.ds(pl.multiple_of(r * step, step), step)
            v = dst[rr, :].astype(F32)
            for s_ in srcs:
                v = v + s_[rr, :].astype(F32)
            dst[rr, :] = v.astype(BF)

    oz = 1 - zl

    class DownSum:
        def push(self, src, dst, i, dev):
            send(src, dst, x_s.at[i], x_r.at[i], dev)

        def part(self, rel):
            xr = ring(x, rel)

            @pl.loop(0, 2)
            def _(z):
                j = xr * 2 + z
                mine = g_all[:, :, pl.ds(pl.multiple_of((2 * j + c) * 256, 256), 256)].reshape(T, 256)
                his = g_sib[:, :, pl.ds(pl.multiple_of(j * 256, 256), 256)].reshape(T, 256)
                xp_d[xr, z] = (dot_nn(act_t[0], mine) + dot_nn(act_s[0], his)).astype(BF)

        def x2(self):
            xr = ring(x, 2)
            self.push(xp_d.at[xr, 0], xh_d.at[0], 0, xdev(1))
            self.push(xp_d.at[xr, 1], xh_d.at[1], 1, xdev(3))

        def x1(self):
            xr = ring(x, 1)
            recv(xh_d.at[0], x_r.at[0], x_s.at[0], xdev(3))
            add_rows(xp_d.at[xr, 0], [xh_d.at[0]], F, 64)
            self.push(xp_d.at[xr], xf_d.at[0], 2, xdev(1))

        def x3(self):
            xr = ring(x, 3)
            recv(xh_d.at[1], x_r.at[1], x_s.at[1], xdev(1))
            add_rows(xp_d.at[xr, 1], [xh_d.at[1]], F, 64)
            self.push(xp_d.at[xr], xf_d.at[1], 3, xdev(3))

        def cross(self):
            recv(xf_d.at[0], x_r.at[2], x_s.at[2], xdev(3))
            recv(xf_d.at[1], x_r.at[3], x_s.at[3], xdev(1))
            add_rows(xp_d.at[x, oz], [xf_d.at[0, oz], xf_d.at[1, oz]], F, 64)
            self.push(xp_d.at[x, oz], xz_d, 4, zsib)

        def fin(self):
            recv(xz_d, x_r.at[4], x_s.at[4], zsib)

            @pl.loop(0, F // 64)
            def _(r):
                rr = pl.ds(pl.multiple_of(r * 64, 64), 64)
                v = xp_d[x, zl, rr, :].astype(F32) + xf_d[0, zl, rr, :].astype(F32)
                v = v + xf_d[1, zl, rr, :].astype(F32) + xz_d[rr, :].astype(F32)
                o_down[rr, :] = v.astype(BF)

    blk = pl.ds(pl.multiple_of(p * 256, 256), 256)

    class WeightSum:
        def push(self, src, dst, i, dev):
            send(src, dst, x_s.at[5 + i], x_r.at[5 + i], dev)

        def get(self, dst, i, dev):
            recv(dst, x_r.at[5 + i], x_s.at[5 + i], dev)

        def part(self, rel):
            xr = ring(x, rel)

            @pl.loop(0, 4)
            def _(i):
                z, k = i // 2, lax.rem(i, 2)
                cols = pl.ds(pl.multiple_of((xr * 2 + z) * 256, 256), 256)
                mine = n_all[c, :, :, cols].reshape(T, 256)
                his = n_all[oc, :, :, cols].reshape(T, 256)
                v = dot_nn(act_t[1 + k], mine) + dot_nn(act_s[1 + k], his)
                xp_w[xr, k, z] = v.astype(BF)

        def x2(self):
            xr = ring(x, 2)
            self.push(xp_w.at[xr, 0], xh_w.at[0], 0, xdev(1))
            self.push(xp_w.at[xr, 1], xh_w.at[1], 1, xdev(3))

        def x1i(self):
            self.push(xp_w.at[ring(x, 1), 1], xf_w.at[0, 1], 2, xdev(1))

        def x3i(self):
            self.push(xp_w.at[ring(x, 3), 0], xf_w.at[1, 0], 3, xdev(3))

        def x1d(self):
            xr = ring(x, 1)
            self.get(xh_w.at[0], 0, xdev(3))
            for z in (oz, zl):
                add_rows(xp_w.at[xr, 0, z], [xh_w.at[0, z]], F, 64)
                self.push(xp_w.at[xr, 0, z], xf_w.at[0, 0, z], 4 if z is oz else 5, xdev(1))

        def x3d(self):
            xr = ring(x, 3)
            self.get(xh_w.at[1], 1, xdev(1))
            for z in (oz, zl):
                add_rows(xp_w.at[xr, 1, z], [xh_w.at[1, z]], F, 64)
                self.push(xp_w.at[xr, 1, z], xf_w.at[1, 1, z], 6 if z is oz else 7, xdev(3))

        def cross(self):
            self.get(xf_w.at[0, 1], 2, xdev(3))
            self.get(xf_w.at[1, 0], 3, xdev(1))
            self.get(xf_w.at[0, 0, oz], 4, xdev(3))
            self.get(xf_w.at[1, 1, oz], 6, xdev(1))
            for k in (0, 1):
                add_rows(xp_w.at[x, k, oz], [xf_w.at[0, k, oz], xf_w.at[1, k, oz]], F, 64)
            self.push(xp_w.at[x, :, oz], xz_w, 8, zsib)

        def fin(self):
            self.get(xf_w.at[0, 0, zl], 5, xdev(3))
            self.get(xf_w.at[1, 1, zl], 7, xdev(1))
            self.get(xz_w, 8, zsib)
            gsum = jnp.zeros((8, 256), F32)
            for k, (o_ref, w_ref) in enumerate(((o_gate, wg), (o_up, wu))):
                def step(r, acc):
                    rr = pl.ds(pl.multiple_of(r * 64, 64), 64)
                    v = xp_w[x, k, zl, rr, :].astype(F32) + xf_w[0, k, zl, rr, :].astype(F32)
                    v = v + xf_w[1, k, zl, rr, :].astype(F32) + xz_w[k, rr, :].astype(F32)
                    o_ref[rr, :] = v.astype(BF)
                    return acc + jnp.sum((v * w_ref[rr, blk].astype(F32)).reshape(8, 8, 256), axis=0)

                gsum = lax.fori_loop(0, F // 64, step, gsum)
            gt[t] = jnp.broadcast_to(jnp.sum(gsum, axis=0, keepdims=True) / vgain[:, blk], (8, 256))
            for k in range(1, 16):
                send(gt.at[t], gt.at[t], g_s.at[0, k], g_r.at[0, k], tdev(k))

    def gain1():
        for k in range(1, 16):
            recv(gt.at[lax.rem(t + 16 - k, 16)], g_r.at[0, k], g_s.at[0, k], tdev(16 - k))
        og[p] = jnp.sum(gt[...], axis=0)
        for k in range(1, 16):
            send(og.at[p], og.at[p], g_s.at[1, k], g_r.at[1, k], pdev(k))

    def gain2():
        for k in range(1, 16):
            recv(og.at[lax.rem(p + 16 - k, 16)], g_r.at[1, k], g_s.at[1, k], pdev(16 - k))
        for k in range(16):
            o_gain[:, pl.ds(k * 256, 256)] = og[k, 0:1, :]

    def p_part(i):
        if "pp" not in begun:
            local[6].wait()
            local[7].wait()
            begun.add("pp")
        cols = pl.ds(i * 512, 512)
        v = dot_nn(acts[0], wg[:, cols]) + dot_nn(acts[1], wu[:, cols])
        part[:, :, cols] = v.astype(BF).reshape(16, 32, 512)

    class Scatter:
        def __init__(self, q, zlast):
            self.cols = pl.ds(q * QW, QW)
            self.zlast = zlast
            self.dev1 = ydev if zlast else zdev
            self.dev2 = zdev if zlast else ydev
            self.s = lambda i: r_s.at[q, i]
            self.r = lambda i: r_r.at[q, i]

        def push(self, src, dst, i, dev):
            send(src, dst, self.s(i), self.r(i), dev)

        def tt(self, k1, k2):
            return tid(k1, k2) if self.zlast else tid(k2, k1)

        def blk(self, k1, k2):
            return part.at[self.tt(k1, k2), :, self.cols]

        def hblk(self, k1, k2, h):
            return part.at[self.tt(k1, k2), pl.ds(16 * h, 16), self.cols]

        def r0(self, k):
            i = KS.index(k)
            self.push(self.hblk(2, k, 0), rh.at[i, 0, :, self.cols], 2 * i, self.dev1(1))
            self.push(self.hblk(2, k, 1), rh.at[i, 1, :, self.cols], 2 * i + 1, self.dev1(3))

        def r1(self, k, h):
            i, k1 = KS.index(k), 1 + 2 * h
            src = rh.at[i, h, :, self.cols]
            recv(src, self.r(2 * i + h), self.s(2 * i + h), self.dev1(4 - k1))
            dst = self.hblk(k1, k, h)
            dst[...] = (dst[...].astype(F32) + src[...].astype(F32)).astype(BF)
            self.push(self.blk(k1, k), rf.at[i, h, :, self.cols], 8 + 2 * i + h, self.dev1(k1))

        def r2(self, k):
            i = KS.index(k)
            for h, k1 in ((0, 3), (1, 1)):
                recv(rf.at[i, h, :, self.cols], self.r(8 + 2 * i + h), self.s(8 + 2 * i + h), self.dev1(k1))
            v = self.blk(0, k)[...].astype(F32) + rf[i, 0, :, self.cols].astype(F32)
            v = v + rf[i, 1, :, self.cols].astype(F32)
            rs[i, :, self.cols] = v.astype(BF)
            if k == 2:
                for h, k2 in ((0, 1), (1, 3)):
                    src = rs.at[i, pl.ds(16 * h, 16), self.cols]
                    self.push(src, zh_buf.at[h, :, self.cols], 16 + h, self.dev2(k2))

        def r4(self, h):
            k2 = 1 + 2 * h
            src = zh_buf.at[h, :, self.cols]
            recv(src, self.r(16 + h), self.s(16 + h), self.dev2(4 - k2))
            i = KS.index(k2)
            dst = rs.at[i, pl.ds(16 * h, 16), self.cols]
            dst[...] = (dst[...].astype(F32) + src[...].astype(F32)).astype(BF)
            self.push(rs.at[i, :, self.cols], zf_buf.at[h, :, self.cols], 18 + h, self.dev2(k2))

        def r5(self):
            for h, k2 in ((0, 3), (1, 1)):
                recv(zf_buf.at[h, :, self.cols], self.r(18 + h), self.s(18 + h), self.dev2(k2))
            v = rs[0, :, self.cols].astype(F32) + zf_buf[0, :, self.cols].astype(F32)
            gn[:, self.cols] = v + zf_buf[1, :, self.cols].astype(F32)

    def finish():
        xin = vin[...].astype(F32)
        inv = lax.rsqrt(jnp.mean(xin * xin, axis=1, keepdims=True) + 1e-05)
        dotp = jnp.zeros((32, 1), F32)
        for q in range(NQ):
            cols = pl.ds(q * QW, QW)
            unit = vin[:, cols].astype(F32) * inv
            dotp = dotp + jnp.sum(gn[:, cols] * vgain[:, cols] * unit, axis=1, keepdims=True)
        dotp = dotp * (1.0 / D)
        for q in range(NQ):
            cols = pl.ds(q * QW, QW)
            unit = vin[:, cols].astype(F32) * inv
            res = g_all[t, :, cols].astype(F32) + inv * (gn[:, cols] * vgain[:, cols] - unit * dotp)
            o_in[:, cols] = res.astype(BF)

    RA = [Scatter(q, MODES["R"][q] == "z") for q in range(NQ)]
    per_quarter = {"G": GA, "N": NA, "R": RA}
    whole = {"D": DownSum(), "W": WeightSum()}
    single = {
        "normed": normed, "nx": nx, "prefac": prefac, "gh": gh_add, "acts": act_grads, "tr": turn, "dready": d_ready,
        "wready": w_ready, "pp": p_part, "gain1": gain1, "gain2": gain2, "fin": finish,
    }
    for name, *rest in ORDER:
        if name in per_quarter:
            step, q, *ks = rest
            getattr(per_quarter[name][q], step)(*ks)
        elif name in whole:
            step, *ks = rest
            getattr(whole[name], step)(*ks)
        else:
            single[name](*rest)
    for cp in sent:
        cp.wait_send()


def deliver(*refs):
    for i in range(5):
        refs[5 + i][...] = refs[i][...]


def body(inputs, gate_pre, up_pre, grad_out, gain, w_gate, w_up, w_down):
    V = pltpu.VMEM
    DMA = pltpu.SemaphoreType.DMA
    any_spec = pl.BlockSpec(memory_space=pl.ANY)
    vm_spec = pl.BlockSpec(memory_space=pltpu.VMEM)
    outs = pl.pallas_call(
        kernel,
        out_shape=(
            jax.ShapeDtypeStruct((32, D), BF),
            jax.ShapeDtypeStruct((F, 256), BF),
            jax.ShapeDtypeStruct((F, 256), BF),
            jax.ShapeDtypeStruct((F, 256), BF),
            jax.ShapeDtypeStruct((1, D), F32),
        ),
        in_specs=[any_spec] * 8,
        out_specs=(vm_spec,) * 5,
        scratch_shapes=[
            V((32, D), BF), V((1, D), F32), V((F, T), BF), V((F, T), BF),
            V((F, D), BF), V((F, D), BF), V((F, D), BF),
            V((16, 32, D), BF), V((16, 32, D // 2), BF), V((2, 16, 32, D // 2), BF), V((32, D // 2), BF),
            V((F, T), F32), V((F, T), F32), V((F, T), F32),
            V((2, T, F), BF), V((3, F, T), BF), V((3, F, T), BF),
            V((16, 32, D), BF), V((4, 2, 16, D), BF), V((4, 2, 32, D), BF), V((4, 32, D), BF),
            V((2, 16, D), BF), V((2, 32, D), BF), V((32, D), F32),
            V((4, 2, F, 256), BF), V((2, F, 256), BF), V((2, 2, F, 256), BF), V((F, 256), BF),
            V((4, 2, 2, F, 256), BF), V((2, 2, F, 256), BF), V((2, 2, 2, F, 256), BF), V((2, F, 256), BF),
            V((16, 8, 256), F32), V((16, 8, 256), F32),
            DMA((8,)), DMA((2, NQ, 20)), DMA((2, NQ, 20)), DMA((NQ, 20)), DMA((NQ, 20)),
            DMA((14,)), DMA((14,)), DMA((12,)), DMA((12,)), DMA((2, 16)), DMA((2, 16)),
        ],
        compiler_params=pltpu.CompilerParams(
            collective_id=0, has_side_effects=True, vmem_limit_bytes=60 * 2**20
        ),
    )(inputs, gate_pre.T, up_pre.T, grad_out, gain.reshape(1, D), w_gate.T, w_up.T, w_down)
    outs = pl.pallas_call(
        deliver,
        out_shape=tuple(jax.ShapeDtypeStruct(o.shape, o.dtype) for o in outs),
        in_specs=[vm_spec] * 5,
        out_specs=(vm_spec,) * 5,
        compiler_params=pltpu.CompilerParams(vmem_limit_bytes=60 * 2**20),
    )(*outs)
    return outs[0], outs[1].T, outs[2].T, outs[3], outs[4].reshape(D)


def solution(mesh):
    return jax.shard_map(
        body,
        mesh=mesh,
        in_specs=(
            P(("dp", "tensor"), None),
            P("dp", "tensor"),
            P("dp", "tensor"),
            P(("dp", "tensor"), None),
            P(),
            P(None, "tensor"),
            P(None, "tensor"),
            P("tensor", None),
        ),
        out_specs=(
            P(("dp", "tensor"), None),
            P("dp", "tensor"),
            P("dp", "tensor"),
            P("tensor", "dp"),
            P(),
        ),
        check_vma=False,
    )
```

time: 432 us -> 134 us (0.31)
  waiting for transfers between devices: 291 us -> 0 us
  Pallas kernels: 0 us -> 133 us
  blocking collectives: 80.4 us -> 0 us
  matrix products: 25.7 us -> 0 us
  other arithmetic: 17.2 us -> 0 us
  between operations: 13.9 us -> 0.64 us
    all_gather x2 -> x0, waiting for transfers between devices: 149 us -> none  [the longest x1 81 us: body(): upstream = lax.all_gather(grad_out, 'tensor', axis=0, tiled=True)]
    reduce_scatter x2 -> x0, waiting for transfers between devices: 141 us -> none  [the longest x1 95.2 us: body(): lax.psum_scatter((jnp.dot(gate_rows, w_gate.T, preferred_element_type=jnp...]
    pallas_call x0 -> x2, Pallas kernels: none -> 133 us  [the longest x1 131 us: body(): pl.pallas_call(kernel, out_shape=(jax.ShapeDtypeStruct((32, D), BF), jax....]
    psum x1 -> x0, blocking collectives: 80.4 us -> none  [body(): lax.psum(jnp.sum(grad_normed * unit_rows, axis=0), ('dp', 'tensor'))]
    dot_general x6 -> x0, matrix products: 25.7 us -> none  [the longest x1 6.18 us: body(): part_down = jnp.dot(upstream.T, hidden, preferred_element_type=jnp.float32)]
    concatenate x1 -> x0, other arithmetic: 14.1 us -> none  [body(): partials = jnp.concatenate([part_gate, part_up, part_down], axis=1)]
  transfers between devices with their start and end apart: 4 -> 0, of which waited for: 4 -> 0; matrix products, arithmetic and copies ran while one was open for 2% -> 0% of each run, Pallas kernels for 0% -> 0%
where the time goes in v2:
time: 134 us
  Pallas kernels  133 us (99%)
    pallas_call x1, Pallas kernels, body(): pl.pallas_call(kernel, out_shape=(jax.ShapeDtypeStruct((32, D), BF), jax....  131 us

profile of v2, /device:TPU:1, one launch (start us, length us, event | category | flops | bytes accessed | tf_op | source)
XLA Modules:
  0.0 133.9 jit_solution(2835059739389690846)
XLA Ops:
  0.6 131.1 %shard_map.119 = (bf16[32,4096]{1,0:T(8,128)(2,1)}, bf16[448,256]{1,0:T(8,128)(2,1)}, bf16[448,256]{1,0:T(8,128)(2,1)}, bf16[448,256]{1,0:T(8,128)(2,1)}, f32[1,4096]{1,0:T(1,128)}) custom-call(bf16[32,4096]{1,0:T(8,128)(2,1)} %inputs.1, bf16[448,512]{1,0:T(8,128)(2,1)} %bitcast.10, bf16[448,512]{1,0:T(8,128)(2,1)} %bitcast.11, bf16[32,4096]{1,0:T(8,128)(2,1)} %grad_out.1, ...), custom_call_target="tpu_custom_call" | custom-call | tf_op jit(solution)/shard_map/pallas_call | solution.py:560
  131.8 2.2 %shard_map.120 = (bf16[32,4096]{1,0:T(8,128)(2,1)}, bf16[448,256]{1,0:T(8,128)(2,1)}, bf16[448,256]{1,0:T(8,128)(2,1)}, bf16[448,256]{1,0:T(8,128)(2,1)}, f32[1,4096]{1,0:T(1,128)}) custom-call(bf16[32,4096]{1,0:T(8,128)(2,1)} %get-tuple-element.15.refs_0_, bf16[448,256]{1,0:T(8,128)(2,1)} %get-tuple-element.16.refs_1_, ...), custom_call_target="tpu_custom_call" | custom-call | tf_op jit(solution)/shard_map/pallas_call | solution.py:589

commit v3 on v2

v3 whole, which is shorter than its diff:
```python
import functools

import jax
import jax.numpy as jnp
from jax import lax
from jax.experimental import pallas as pl
from jax.experimental.pallas import tpu as pltpu
from jax.sharding import PartitionSpec as P

MESH = pl.DeviceIdType.MESH
BF = jnp.bfloat16
F32 = jnp.float32
D = 4096
F = 448
T = 512
NQ = 4
QW = D // NQ
KS = (0, 1, 3, 2)
MODES = {'G': 'zzzz', 'N': 'zzyz', 'R': 'zzzy'}
ORDER = (
    ('G', 'e0', 0), ('G', 'e0', 2), ('G', 's2', 2, 0), ('G', 's2', 0, 0), ('G', 'e0', 1), ('G', 's2', 1, 0),
    ('prefac',), ('normed',), ('hx',), ('nx',), ('N', 'e0', 2), ('G', 'e0', 3), ('G', 's2', 3, 0),
    ('G', 'f2', 2, 0, 3), ('G', 'f2', 2, 0, 1), ('G', 'f1', 0, 3), ('G', 'f1', 0, 1), ('G', 's2', 0, 3),
    ('G', 's2', 0, 1), ('G', 'f2', 0, 0, 3), ('G', 'f2', 0, 0, 1), ('G', 'f2', 1, 0, 3), ('G', 'f2', 1, 0, 1),
    ('G', 'f1', 2, 3), ('G', 's2', 2, 3), ('G', 'f1', 2, 1), ('N', 'f1', 2, 3), ('N', 'f1', 2, 1),
    ('G', 'f2', 3, 0, 3), ('G', 'f2', 3, 0, 1), ('G', 's2', 2, 1), ('G', 'f1', 1, 3), ('G', 'f1', 1, 1),
    ('G', 'f2', 0, 3, 3), ('G', 'f2', 0, 3, 1), ('N', 'e0', 3), ('G', 's2', 1, 3), ('G', 'f2', 0, 1, 3),
    ('G', 'f2', 0, 1, 1), ('G', 'f1', 3, 3), ('G', 'f1', 3, 1), ('G', 's2', 1, 1), ('G', 'e3', 0), ('G', 's2', 0, 2),
    ('G', 'f2', 2, 3, 3), ('G', 'f2', 2, 3, 1), ('N', 'e0', 1), ('G', 'e3', 2), ('N', 'e3', 2), ('G', 'e3', 1),
    ('G', 's2', 1, 2), ('G', 'f2', 2, 1, 3), ('G', 'f2', 2, 1, 1), ('N', 'e0', 0), ('G', 's2', 2, 2),
    ('N', 'f1', 3, 3), ('N', 'f1', 3, 1), ('G', 'f2', 1, 3, 3), ('G', 'f2', 1, 3, 1), ('G', 'e3', 3),
    ('G', 's2', 3, 3), ('G', 'f2', 1, 1, 3), ('G', 'f2', 1, 1, 1), ('N', 's2', 2, 0), ('G', 'f2', 0, 2, 3),
    ('G', 'f2', 0, 2, 1), ('N', 'f1', 1, 3), ('N', 'f1', 1, 1), ('G', 's2', 3, 1), ('G', 'f2', 1, 2, 3),
    ('G', 'f2', 1, 2, 1), ('G', 's2', 3, 2), ('N', 'f1', 0, 3), ('N', 'f1', 0, 1), ('G', 'f2', 2, 2, 3),
    ('G', 'f2', 2, 2, 1), ('N', 's2', 2, 3), ('N', 'e3', 3), ('N', 's2', 0, 0), ('G', 'f2', 3, 3, 3),
    ('G', 'f2', 3, 3, 1), ('N', 'f2', 2, 0, 3), ('N', 'f2', 2, 0, 1), ('N', 's2', 0, 3), ('G', 'done', 0), ('gh', 0),
    ('N', 's2', 2, 1), ('N', 'e3', 1), ('N', 's2', 0, 1), ('G', 'f2', 3, 1, 3), ('G', 'f2', 3, 1, 1),
    ('G', 'done', 1), ('gh', 1), ('dr', 0), ('D', 'part', 2), ('G', 'f2', 3, 2, 3), ('G', 'f2', 3, 2, 1), ('D', 'x2'),
    ('G', 'done', 2), ('N', 's2', 1, 0), ('N', 'e3', 0), ('N', 's2', 2, 2), ('gh', 2), ('dr', 1), ('D', 'part', 1),
    ('N', 's2', 0, 2), ('N', 'f2', 0, 0, 3), ('N', 'f2', 0, 0, 1), ('N', 'f2', 2, 3, 3), ('N', 'f2', 2, 3, 1),
    ('dr', 2), ('D', 'part', 3), ('N', 'f2', 0, 3, 3), ('N', 'f2', 0, 3, 1), ('N', 's2', 1, 3), ('N', 'f2', 0, 1, 3),
    ('N', 'f2', 0, 1, 1), ('N', 'f2', 2, 1, 3), ('N', 'f2', 2, 1, 1), ('N', 's2', 1, 1), ('G', 'done', 3), ('gh', 3),
    ('acts',), ('tr',), ('pp', 6), ('D', 'x1'), ('D', 'x3'), ('pp', 7), ('N', 'f2', 0, 2, 3), ('N', 'f2', 0, 2, 1),
    ('N', 's2', 1, 2), ('N', 'f2', 2, 2, 3), ('N', 'f2', 2, 2, 1), ('pp', 2), ('wready',), ('N', 'f2', 1, 0, 3),
    ('N', 'f2', 1, 0, 1), ('pp', 1), ('N', 'f2', 1, 3, 3), ('N', 'f2', 1, 3, 1), ('R', 'r0', 3, 2), ('R', 'r0', 3, 1),
    ('R', 'r0', 3, 3), ('R', 'r0', 3, 0), ('N', 's2', 3, 0), ('pp', 0), ('N', 's2', 3, 3), ('R', 'r0', 0, 2),
    ('pp', 3), ('N', 'f2', 1, 1, 3), ('N', 'f2', 1, 1, 1), ('dr', 3), ('D', 'part', 0), ('N', 'done', 0),
    ('W', 'part', 2), ('W', 'x2'), ('N', 'f2', 1, 2, 3), ('N', 'f2', 1, 2, 1), ('R', 'r1', 3, 2, 0),
    ('R', 'r1', 3, 2, 1), ('N', 's2', 3, 1), ('N', 's2', 3, 2), ('N', 'done', 2), ('W', 'part', 3), ('W', 'x3i'),
    ('N', 'f2', 3, 0, 3), ('N', 'f2', 3, 0, 1), ('R', 'r1', 3, 1, 0), ('R', 'r1', 3, 1, 1), ('R', 'r1', 3, 3, 0),
    ('R', 'r1', 3, 3, 1), ('R', 'r0', 0, 1), ('N', 'f2', 3, 3, 3), ('N', 'f2', 3, 3, 1), ('R', 'r0', 0, 3), ('pp', 4),
    ('R', 'r1', 3, 0, 0), ('R', 'r1', 3, 0, 1), ('R', 'r0', 0, 0), ('R', 'r0', 1, 2), ('R', 'r1', 0, 2, 0),
    ('R', 'r1', 0, 2, 1), ('D', 'cross'), ('pp', 5), ('N', 'done', 1), ('W', 'part', 1), ('N', 'f2', 3, 1, 3),
    ('N', 'f2', 3, 1, 1), ('R', 'r2', 3, 2), ('R', 'r0', 2, 2), ('W', 'x1i'), ('N', 'f2', 3, 2, 3),
    ('N', 'f2', 3, 2, 1), ('R', 'r2', 3, 1), ('R', 'r0', 2, 1), ('R', 'r1', 0, 1, 0), ('R', 'r1', 0, 1, 1),
    ('R', 'r1', 0, 3, 0), ('R', 'r1', 0, 3, 1), ('R', 'r1', 0, 0, 0), ('R', 'r1', 0, 0, 1), ('R', 'r2', 3, 3),
    ('R', 'r1', 1, 2, 0), ('R', 'r1', 1, 2, 1), ('R', 'r2', 0, 2), ('W', 'x1d'), ('W', 'x3d'), ('R', 'r2', 3, 0),
    ('R', 'r4', 3, 0), ('R', 'r4', 3, 1), ('R', 'r1', 2, 2, 0), ('R', 'r1', 2, 2, 1), ('N', 'done', 3),
    ('W', 'part', 0), ('R', 'r0', 2, 3), ('R', 'r1', 2, 1, 0), ('R', 'r1', 2, 1, 1), ('R', 'r2', 0, 1), ('D', 'fin'),
    ('R', 'r2', 0, 3), ('R', 'r0', 2, 0), ('R', 'r4', 0, 0), ('R', 'r4', 0, 1), ('R', 'r0', 1, 1), ('R', 'r2', 0, 0),
    ('R', 'r0', 1, 3), ('R', 'r0', 1, 0), ('R', 'r2', 1, 2), ('R', 'r5', 3), ('W', 'cross'), ('R', 'r2', 2, 2),
    ('R', 'r1', 2, 3, 0), ('R', 'r1', 2, 3, 1), ('R', 'r5', 0), ('R', 'r2', 2, 1), ('R', 'r1', 2, 0, 0),
    ('R', 'r1', 2, 0, 1), ('R', 'r1', 1, 1, 0), ('R', 'r1', 1, 1, 1), ('R', 'r1', 1, 3, 0), ('R', 'r1', 1, 3, 1),
    ('R', 'r1', 1, 0, 0), ('R', 'r1', 1, 0, 1), ('R', 'r2', 2, 3), ('R', 'r2', 2, 0), ('W', 'own'), ('R', 'r2', 1, 1),
    ('R', 'r4', 1, 0), ('R', 'r2', 1, 3), ('R', 'r4', 1, 1), ('R', 'r2', 1, 0), ('W', 'fin'), ('R', 'r4', 2, 0),
    ('R', 'r4', 2, 1), ('gain1',), ('R', 'r5', 1), ('R', 'r5', 2), ('fin',), ('gain2',),
)
RELS = (2, 1, 3, 0)


def dot_nt(a, b):
    return lax.dot_general(a, b, (((1,), (1,)), ((), ())), preferred_element_type=F32)


def dot_nn(a, b):
    return lax.dot_general(a, b, (((1,), (0,)), ((), ())), preferred_element_type=F32)


def kernel(
    inputs, gate_pre, up_pre, grad_out, gain, w_gate, w_up, w_down,
    o_in, o_gate, o_up, o_down, o_gain,
    vin, vgain, vgp, vup, wg, wu, wd,
    g_all, g_sib, n_all, n_send, a1, a2, gh, acts, act_t, act_s,
    part, rh, rf, rs, zh_buf, zf_buf, gn,
    xp_d, xh_d, xf_d, xz_d, xp_w, xh_w, xf_w, xz_w,
    gt, og,
    loc, ag_s, ag_r, r_s, r_r, x_s, x_r, c_s, c_r, g_s, g_r,
):
    p = lax.axis_index("dp")
    t = lax.axis_index("tensor")
    x, zl, c = p // 4, lax.rem(p // 2, 2), lax.rem(p, 2)
    y, zh = t // 4, lax.rem(t, 4)
    oc = 1 - c
    sib = (x * 4 + zl * 2 + oc, t)
    zsib = (x * 4 + (1 - zl) * 2 + c, t)

    def ring(v, k):
        return lax.rem(v + k, 4)

    def ydev(k):
        return (p, ring(y, k) * 4 + zh)

    def zdev(k):
        return (p, y * 4 + ring(zh, k))

    def xdev(k):
        return (ring(x, k) * 4 + zl * 2 + c, t)

    def tdev(k):
        return (p, lax.rem(t + k, 16))

    def pdev(k):
        return (lax.rem(p + k, 16), t)

    def tid(ky, kz):
        return ring(y, ky) * 4 + ring(zh, kz)

    sent = []

    def send(src, dst, ss, rs_, dev):
        cp = pltpu.make_async_remote_copy(
            src_ref=src, dst_ref=dst, send_sem=ss, recv_sem=rs_, device_id=dev, device_id_type=MESH
        )
        cp.start()
        return cp

    def wait_sent(ref, sem, dev):
        pltpu.make_async_remote_copy(
            src_ref=ref, dst_ref=ref, send_sem=sem, recv_sem=sem, device_id=dev, device_id_type=MESH
        ).wait_send()

    def recv(dst, sem, ss, dev):
        pltpu.make_async_remote_copy(
            src_ref=dst, dst_ref=dst, send_sem=ss, recv_sem=sem, device_id=dev, device_id_type=MESH
        ).wait_recv()

    barrier = pltpu.get_barrier_semaphore()
    partners = [f(k) for f in (ydev, zdev, xdev) for k in (1, 3)] + [sib, zsib]
    for dev in partners:
        pl.semaphore_signal(barrier, inc=1, device_id=dev, device_id_type=MESH)
    local = []
    for i, (src, dst) in enumerate((
        (inputs, vin), (gain, vgain), (gate_pre, vgp), (up_pre, vup),
        (grad_out, g_all.at[t]), (w_down, wd), (w_gate, wg), (w_up, wu),
    )):
        cp = pltpu.make_async_copy(src, dst, loc.at[i])
        cp.start()
        local.append(cp)

    local[0].wait()
    local[1].wait()
    xin = vin[...].astype(F32)
    inv = lax.rsqrt(jnp.mean(xin * xin, axis=1, keepdims=True) + 1e-05)

    @pl.loop(0, 8)
    def _(j):
        own = pl.ds(pl.multiple_of((2 * j + c) * 256, 256), 256)
        oth = pl.ds(pl.multiple_of((2 * j + oc) * 256, 256), 256)
        col = pl.ds(pl.multiple_of(j * 256, 256), 256)
        n_all[c, t, :, col] = (vin[:, own].astype(F32) * inv * vgain[:, own]).astype(BF)
        n_send[:, col] = (vin[:, oth].astype(F32) * inv * vgain[:, oth]).astype(BF)
    pl.semaphore_wait(barrier, len(partners))

    class Gather:
        def __init__(self, item, q, zfirst, piece, half, group, own):
            self.piece_t, self.half_t, self.group_t, self.own = piece, half, group, own
            self.zfirst = zfirst
            self.sem = ag_s.at[item, q]
            self.s = lambda i: self.sem
            self.r = lambda i: ag_r.at[item, q, i]
            self.dev1 = zdev if zfirst else ydev
            self.dev2 = ydev if zfirst else zdev

        def tt(self, ku, kv):
            return tid(kv, ku) if self.zfirst else tid(ku, kv)

        def piece(self, ku, kv):
            return self.piece_t(self.tt(ku, kv))

        def half(self, ku, kv, h):
            return self.half_t(self.tt(ku, kv), h)

        def push(self, src, dst, i, dev):
            send(src, dst, self.s(i), self.r(i), dev)

        def e0(self):
            ref = self.piece(0, 0)
            src = ref if self.own is None else self.own
            self.push(src, ref, 1, self.dev1(1))
            self.push(src, ref, 0, self.dev1(3))

        def s2(self, k):
            i = KS.index(k)
            ref = self.piece(k, 0)
            src = ref if self.own is None or k else self.own
            self.push(src, ref, 3 + 2 * i + 1, self.dev2(1))
            self.push(src, ref, 3 + 2 * i, self.dev2(3))

        def f1(self, k):
            h = k // 2
            recv(self.piece(k, 0), self.r(h), self.s(h), self.dev1(k))
            self.push(self.half(k, 0, h), self.half(k, 0, h), 2, self.dev1(4 - k))

        def f2(self, k, kk):
            i, h = KS.index(k), kk // 2
            recv(self.piece(k, kk), self.r(3 + 2 * i + h), self.sem, self.dev2(kk))
            self.push(self.half(k, kk, h), self.half(k, kk, h), 11, self.dev2(4 - kk))

        def e3(self):
            recv(self.piece(2, 0), self.r(2), self.sem, self.dev1(1))

        def done(self):
            recv(self.group_t(4), self.r(11), self.sem, self.dev2(1))

        def settle(self):
            wait_sent(self.group_t(15), self.sem, self.dev1(1))

    def g_cols(q):
        return pl.ds(pl.multiple_of(ring(x, RELS[q]) * QW, QW), QW)

    def n_cols(q):
        return pl.ds(pl.multiple_of(ring(x, RELS[q]) * 512, 512), 512)

    GA = [
        Gather(
            0, q, MODES['G'][q] == 'z',
            lambda tt, q=q: g_all.at[tt, :, g_cols(q)],
            lambda tt, h, q=q: g_all.at[tt, pl.ds(16 * h, 16), g_cols(q)],
            lambda n, q=q: g_all.at[pl.ds(0, n), :, g_cols(q)],
            grad_out.at[:, g_cols(q)],
        )
        for q in range(NQ)
    ]
    NA = [
        Gather(
            1, q, MODES['N'][q] == 'z',
            lambda tt, q=q: n_all.at[:, tt, :, n_cols(q)],
            lambda tt, h, q=q: n_all.at[h, tt, :, n_cols(q)],
            lambda n, q=q: n_all.at[:, pl.ds(0, n), :, n_cols(q)],
            None,
        )
        for q in range(NQ)
    ]

    def normed():
        sent.append(send(n_send, n_all.at[c, t], c_s.at[0], c_r.at[0], sib))

    def nx():
        recv(n_all.at[oc, t], c_r.at[0], c_s.at[0], sib)

    def prefac():
        local[2].wait()
        local[3].wait()

        @pl.loop(0, F // 64)
        def _(r):
            rows = pl.ds(pl.multiple_of(r * 64, 64), 64)
            gp = vgp[rows, :].astype(F32)
            up = vup[rows, :].astype(F32)
            s = jax.nn.sigmoid(gp)
            gs = gp * s
            a2[rows, :] = gs
            a1[rows, :] = up * (s * (1.0 + gp * (1.0 - s)))
            act_t[0, rows, :] = (gs * up).astype(BF)

        sent.append(send(act_t.at[0], act_s.at[0], c_s.at[1], c_r.at[1], sib))

    begun = set()

    def gh_add(q):
        if "gh" not in begun:
            local[4].wait()
            local[5].wait()
        v = dot_nt(wd[:, g_cols(q)], g_all[:, :, g_cols(q)].reshape(T, QW))
        gh[...] = v if "gh" not in begun else gh[...] + v
        begun.add("gh")
        for i in range(2):
            j = 2 * ring(x, RELS[q]) + i
            src = g_all.at[:, :, pl.ds(pl.multiple_of((2 * j + oc) * 256, 256), 256)]
            dst = g_sib.at[:, :, pl.ds(pl.multiple_of(j * 256, 256), 256)]
            sent.append(send(src, dst, c_s.at[4 + 2 * q + i], c_r.at[4 + 2 * q + i], sib))

    def act_grads():
        @pl.loop(0, F // 64)
        def _(r):
            rows = pl.ds(pl.multiple_of(r * 64, 64), 64)
            v = gh[rows, :]
            act_t[1, rows, :] = (v * a1[rows, :]).astype(BF)
            act_t[2, rows, :] = (v * a2[rows, :]).astype(BF)

        for i in (1, 2):
            sent.append(send(act_t.at[i], act_s.at[i], c_s.at[1 + i], c_r.at[1 + i], sib))

    def turn():
        @pl.loop(0, 4)
        def _(r):
            rows = pl.ds(pl.multiple_of(r * 128, 128), 128)
            for i in (1, 2):
                acts[i - 1, rows, :] = act_t[i, :, rows].T

    def h_ready():
        recv(act_s.at[0], c_r.at[1], c_s.at[1], sib)

    def d_ready(q):
        for i in range(2):
            j = 2 * ring(x, RELS[q]) + i
            dst = g_sib.at[:, :, pl.ds(pl.multiple_of(j * 256, 256), 256)]
            recv(dst, c_r.at[4 + 2 * q + i], c_s.at[4 + 2 * q + i], sib)

    def w_ready():
        for i in (1, 2):
            recv(act_s.at[i], c_r.at[1 + i], c_s.at[1 + i], sib)

    def add_rows(dst, srcs, rows, step):
        @pl.loop(0, rows // step)
        def _(r):
            rr = pl.ds(pl.multiple_of(r * step, step), step)
            v = dst[rr, :].astype(F32)
            for s_ in srcs:
                v = v + s_[rr, :].astype(F32)
            dst[rr, :] = v.astype(BF)

    oz = 1 - zl

    class DownSum:
        def push(self, src, dst, i, dev):
            sent.append(send(src, dst, x_s.at[i], x_r.at[i], dev))

        def part(self, rel):
            xr = ring(x, rel)

            @pl.loop(0, 2)
            def _(z):
                j = xr * 2 + z
                mine = g_all[:, :, pl.ds(pl.multiple_of((2 * j + c) * 256, 256), 256)].reshape(T, 256)
                his = g_sib[:, :, pl.ds(pl.multiple_of(j * 256, 256), 256)].reshape(T, 256)
                xp_d[xr, z] = (dot_nn(act_t[0], mine) + dot_nn(act_s[0], his)).astype(BF)

        def x2(self):
            xr = ring(x, 2)
            self.push(xp_d.at[xr, 0], xh_d.at[0], 0, xdev(1))
            self.push(xp_d.at[xr, 1], xh_d.at[1], 1, xdev(3))

        def x1(self):
            xr = ring(x, 1)
            recv(xh_d.at[0], x_r.at[0], x_s.at[0], xdev(3))
            add_rows(xp_d.at[xr, 0], [xh_d.at[0]], F, 64)
            self.push(xp_d.at[xr], xf_d.at[0], 2, xdev(1))

        def x3(self):
            xr = ring(x, 3)
            recv(xh_d.at[1], x_r.at[1], x_s.at[1], xdev(1))
            add_rows(xp_d.at[xr, 1], [xh_d.at[1]], F, 64)
            self.push(xp_d.at[xr], xf_d.at[1], 3, xdev(3))

        def cross(self):
            recv(xf_d.at[0], x_r.at[2], x_s.at[2], xdev(3))
            recv(xf_d.at[1], x_r.at[3], x_s.at[3], xdev(1))
            add_rows(xp_d.at[x, oz], [xf_d.at[0, oz], xf_d.at[1, oz]], F, 64)
            self.push(xp_d.at[x, oz], xz_d, 4, zsib)

        def fin(self):
            recv(xz_d, x_r.at[4], x_s.at[4], zsib)

            @pl.loop(0, F // 64)
            def _(r):
                rr = pl.ds(pl.multiple_of(r * 64, 64), 64)
                v = xp_d[x, zl, rr, :].astype(F32) + xf_d[0, zl, rr, :].astype(F32)
                v = v + xf_d[1, zl, rr, :].astype(F32) + xz_d[rr, :].astype(F32)
                o_down[rr, :] = v.astype(BF)


    class WeightSum:
        def push(self, src, dst, i, dev):
            sent.append(send(src, dst, x_s.at[5 + i], x_r.at[5 + i], dev))

        def get(self, dst, i, dev):
            recv(dst, x_r.at[5 + i], x_s.at[5 + i], dev)

        def part(self, rel):
            xr = ring(x, rel)

            @pl.loop(0, 4)
            def _(i):
                z, k = i // 2, lax.rem(i, 2)
                cols = pl.ds(pl.multiple_of((xr * 2 + z) * 256, 256), 256)
                mine = n_all[c, :, :, cols].reshape(T, 256)
                his = n_all[oc, :, :, cols].reshape(T, 256)
                v = dot_nn(act_t[1 + k], mine) + dot_nn(act_s[1 + k], his)
                xp_w[xr, k, z] = v.astype(BF)

        def x2(self):
            xr = ring(x, 2)
            self.push(xp_w.at[xr, 0], xh_w.at[0], 0, xdev(1))
            self.push(xp_w.at[xr, 1], xh_w.at[1], 1, xdev(3))

        def x1i(self):
            self.push(xp_w.at[ring(x, 1), 1, oz], xf_w.at[0, 1, oz], 2, xdev(1))

        def x3i(self):
            self.push(xp_w.at[ring(x, 3), 0, oz], xf_w.at[1, 0, oz], 3, xdev(3))

        def x1d(self):
            xr = ring(x, 1)
            self.get(xh_w.at[0], 0, xdev(3))
            add_rows(xp_w.at[xr, 0, oz], [xh_w.at[0, oz]], F, 64)
            self.push(xp_w.at[xr, 0, oz], xf_w.at[0, 0, oz], 4, xdev(1))
            self.push(xp_w.at[xr, 1, zl], xf_w.at[0, 1, zl], 9, xdev(1))
            add_rows(xp_w.at[xr, 0, zl], [xh_w.at[0, zl]], F, 64)
            self.push(xp_w.at[xr, 0, zl], xf_w.at[0, 0, zl], 5, xdev(1))

        def x3d(self):
            xr = ring(x, 3)
            self.get(xh_w.at[1], 1, xdev(1))
            add_rows(xp_w.at[xr, 1, oz], [xh_w.at[1, oz]], F, 64)
            self.push(xp_w.at[xr, 1, oz], xf_w.at[1, 1, oz], 6, xdev(3))
            self.push(xp_w.at[xr, 0, zl], xf_w.at[1, 0, zl], 10, xdev(3))
            add_rows(xp_w.at[xr, 1, zl], [xh_w.at[1, zl]], F, 64)
            self.push(xp_w.at[xr, 1, zl], xf_w.at[1, 1, zl], 7, xdev(3))

        def gather_sum(self, z):
            cols = pl.ds(pl.multiple_of((x * 4 + z * 2 + c) * 256, 256), 256)
            gsum = jnp.zeros((8, 256), F32)
            for k, w_ref in enumerate((wg, wu)):
                def step(r, acc):
                    rr = pl.ds(pl.multiple_of(r * 64, 64), 64)
                    v = xp_w[x, k, z, rr, :].astype(F32) + xf_w[0, k, z, rr, :].astype(F32)
                    v = v + xf_w[1, k, z, rr, :].astype(F32)
                    xp_w[x, k, z, rr, :] = v.astype(BF)
                    return acc + jnp.sum((v * w_ref[rr, cols].astype(F32)).reshape(8, 8, 256), axis=0)

                gsum = lax.fori_loop(0, F // 64, step, gsum)
            gt[t, pl.ds(z, 1), :] = jnp.sum(gsum, axis=0, keepdims=True) / vgain[:, cols]

        def cross(self):
            self.get(xf_w.at[0, 1, oz], 2, xdev(3))
            self.get(xf_w.at[1, 0, oz], 3, xdev(1))
            self.get(xf_w.at[0, 0, oz], 4, xdev(3))
            self.get(xf_w.at[1, 1, oz], 6, xdev(1))
            gt[t] = jnp.zeros((8, 256), F32)
            self.gather_sum(oz)
            self.push(xp_w.at[x, :, oz], xz_w, 8, zsib)

        def own(self):
            self.get(xf_w.at[0, 1, zl], 9, xdev(3))
            self.get(xf_w.at[1, 0, zl], 10, xdev(1))
            self.get(xf_w.at[0, 0, zl], 5, xdev(3))
            self.get(xf_w.at[1, 1, zl], 7, xdev(1))
            self.gather_sum(zl)
            for k in range(1, 16):
                send(gt.at[t], gt.at[t], g_s.at[0], g_r.at[0], tdev(k))

        def fin(self):
            self.get(xz_w, 8, zsib)
            for k, o_ref in enumerate((o_gate, o_up)):
                @pl.loop(0, F // 64)
                def _(r):
                    rr = pl.ds(pl.multiple_of(r * 64, 64), 64)
                    o_ref[rr, :] = (xp_w[x, k, zl, rr, :].astype(F32) + xz_w[k, rr, :].astype(F32)).astype(BF)


    def gain1():
        recv(gt.at[pl.ds(0, 15)], g_r.at[0], g_s.at[0], tdev(1))
        og[p] = jnp.sum(gt[...], axis=0)
        for k in range(1, 16):
            send(og.at[p], og.at[p], g_s.at[1], g_r.at[1], pdev(k))

    def gain2():
        recv(og.at[pl.ds(0, 15)], g_r.at[1], g_s.at[1], pdev(1))
        for k in range(16):
            z, k0 = (k // 2) % 2, k - k % 4 + k % 2
            o_gain[:, pl.ds(k * 256, 256)] = og[k0, z : z + 1, :] + og[k0 + 2, z : z + 1, :]

    def p_part(i):
        if "pp" not in begun:
            local[6].wait()
            local[7].wait()
            begun.add("pp")
        cols = pl.ds(i * 512, 512)
        v = dot_nn(acts[0], wg[:, cols]) + dot_nn(acts[1], wu[:, cols])
        part[:, :, cols] = v.astype(BF).reshape(16, 32, 512)

    class Scatter:
        def __init__(self, q, zlast):
            self.cols = pl.ds(q * QW, QW)
            self.zlast = zlast
            self.dev1 = ydev if zlast else zdev
            self.dev2 = zdev if zlast else ydev
            self.sem = r_s.at[q]
            self.s = lambda i: self.sem
            self.r = lambda i: r_r.at[q, i]

        def push(self, src, dst, i, dev):
            send(src, dst, self.s(i), self.r(i), dev)

        def tt(self, k1, k2):
            return tid(k1, k2) if self.zlast else tid(k2, k1)

        def blk(self, k1, k2):
            return part.at[self.tt(k1, k2), :, self.cols]

        def hblk(self, k1, k2, h):
            return part.at[self.tt(k1, k2), pl.ds(16 * h, 16), self.cols]

        def r0(self, k):
            i = KS.index(k)
            self.push(self.hblk(2, k, 0), rh.at[i, 0, :, self.cols], 2 * i, self.dev1(1))
            self.push(self.hblk(2, k, 1), rh.at[i, 1, :, self.cols], 2 * i + 1, self.dev1(3))

        def r1(self, k, h):
            i, k1 = KS.index(k), 1 + 2 * h
            src = rh.at[i, h, :, self.cols]
            recv(src, self.r(2 * i + h), self.s(2 * i + h), self.dev1(4 - k1))
            dst = self.hblk(k1, k, h)
            dst[...] = (dst[...].astype(F32) + src[...].astype(F32)).astype(BF)
            self.push(self.blk(k1, k), rf.at[i, h, :, self.cols], 8 + i, self.dev1(k1))

        def r2(self, k):
            i = KS.index(k)
            recv(rf.at[i, :, :, self.cols], self.r(8 + i), self.sem, self.dev1(1))
            v = self.blk(0, k)[...].astype(F32) + rf[i, 0, :, self.cols].astype(F32)
            v = v + rf[i, 1, :, self.cols].astype(F32)
            rs[i, :, self.cols] = v.astype(BF)
            if k == 2:
                for h, k2 in ((0, 1), (1, 3)):
                    src = rs.at[i, pl.ds(16 * h, 16), self.cols]
                    self.push(src, zh_buf.at[h, :, self.cols], 12 + h, self.dev2(k2))

        def r4(self, h):
            k2 = 1 + 2 * h
            src = zh_buf.at[h, :, self.cols]
            recv(src, self.r(12 + h), self.sem, self.dev2(4 - k2))
            i = KS.index(k2)
            dst = rs.at[i, pl.ds(16 * h, 16), self.cols]
            dst[...] = (dst[...].astype(F32) + src[...].astype(F32)).astype(BF)
            self.push(rs.at[i, :, self.cols], zf_buf.at[h, :, self.cols], 14, self.dev2(k2))

        def r5(self):
            recv(zf_buf.at[:, :, self.cols], self.r(14), self.sem, self.dev2(1))
            v = rs[0, :, self.cols].astype(F32) + zf_buf[0, :, self.cols].astype(F32)
            gn[:, self.cols] = v + zf_buf[1, :, self.cols].astype(F32)

        def settle(self):
            wait_sent(part.at[pl.ds(0, 15), :, self.cols], self.sem, self.dev1(1))

    def finish():
        xin = vin[...].astype(F32)
        inv = lax.rsqrt(jnp.mean(xin * xin, axis=1, keepdims=True) + 1e-05)
        dotp = jnp.zeros((32, 1), F32)
        for q in range(NQ):
            cols = pl.ds(q * QW, QW)
            unit = vin[:, cols].astype(F32) * inv
            dotp = dotp + jnp.sum(gn[:, cols] * vgain[:, cols] * unit, axis=1, keepdims=True)
        dotp = dotp * (1.0 / D)
        for q in range(NQ):
            cols = pl.ds(q * QW, QW)
            unit = vin[:, cols].astype(F32) * inv
            res = g_all[t, :, cols].astype(F32) + inv * (gn[:, cols] * vgain[:, cols] - unit * dotp)
            o_in[:, cols] = res.astype(BF)

    RA = [Scatter(q, MODES["R"][q] == "z") for q in range(NQ)]
    per_quarter = {"G": GA, "N": NA, "R": RA}
    whole = {"D": DownSum(), "W": WeightSum()}
    single = {
        "normed": normed, "nx": nx, "prefac": prefac, "gh": gh_add, "acts": act_grads, "tr": turn, "hx": h_ready, "dr": d_ready,
        "wready": w_ready, "pp": p_part, "gain1": gain1, "gain2": gain2, "fin": finish,
    }
    for name, *rest in ORDER:
        if name in per_quarter:
            step, q, *ks = rest
            getattr(per_quarter[name][q], step)(*ks)
        elif name in whole:
            step, *ks = rest
            getattr(whole[name], step)(*ks)
        else:
            single[name](*rest)
    for q in range(NQ):
        GA[q].settle()
        NA[q].settle()
        RA[q].settle()
    wait_sent(gt.at[pl.ds(0, 15)], g_s.at[0], tdev(1))
    wait_sent(og.at[pl.ds(0, 15)], g_s.at[1], pdev(1))
    for cp in sent:
        cp.wait_send()


def deliver(*refs):
    copies = [pltpu.make_async_copy(refs[i], refs[5 + i], refs[10].at[i]) for i in range(5)]
    for cp in copies:
        cp.start()
    for cp in copies:
        cp.wait()


def body(inputs, gate_pre, up_pre, grad_out, gain, w_gate, w_up, w_down):
    V = pltpu.VMEM
    DMA = pltpu.SemaphoreType.DMA
    any_spec = pl.BlockSpec(memory_space=pl.ANY)
    vm_spec = pl.BlockSpec(memory_space=pltpu.VMEM)
    outs = pl.pallas_call(
        kernel,
        out_shape=(
            V((32, D), BF),
            V((F, 256), BF),
            V((F, 256), BF),
            V((F, 256), BF),
            V((1, D), F32),
        ),
        in_specs=[any_spec] * 8,
        out_specs=(vm_spec,) * 5,
        scratch_shapes=[
            V((32, D), BF), V((1, D), F32), V((F, T), BF), V((F, T), BF),
            V((F, D), BF), V((F, D), BF), V((F, D), BF),
            V((16, 32, D), BF), V((16, 32, D // 2), BF), V((2, 16, 32, D // 2), BF), V((32, D // 2), BF),
            V((F, T), F32), V((F, T), F32), V((F, T), F32),
            V((2, T, F), BF), V((3, F, T), BF), V((3, F, T), BF),
            V((16, 32, D), BF), V((4, 2, 16, D), BF), V((4, 2, 32, D), BF), V((4, 32, D), BF),
            V((2, 16, D), BF), V((2, 32, D), BF), V((32, D), F32),
            V((4, 2, F, 256), BF), V((2, F, 256), BF), V((2, 2, F, 256), BF), V((F, 256), BF),
            V((4, 2, 2, F, 256), BF), V((2, 2, F, 256), BF), V((2, 2, 2, F, 256), BF), V((2, F, 256), BF),
            V((16, 8, 256), F32), V((16, 8, 256), F32),
            DMA((8,)), DMA((2, NQ)), DMA((2, NQ, 12)), DMA((NQ,)), DMA((NQ, 15)),
            DMA((16,)), DMA((16,)), DMA((12,)), DMA((12,)), DMA((2,)), DMA((2,)),
        ],
        compiler_params=pltpu.CompilerParams(
            collective_id=0, has_side_effects=True, vmem_limit_bytes=56 * 2**20
        ),
    )(inputs, gate_pre.T, up_pre.T, grad_out, gain.reshape(1, D), w_gate.T, w_up.T, w_down)
    outs = pl.pallas_call(
        deliver,
        out_shape=tuple(jax.ShapeDtypeStruct(o.shape, o.dtype) for o in outs),
        in_specs=[vm_spec] * 5,
        out_specs=(any_spec,) * 5,
        scratch_shapes=[DMA((5,))],
        compiler_params=pltpu.CompilerParams(vmem_limit_bytes=40 * 2**20),
    )(*[pltpu.with_memory_space_constraint(o, pltpu.VMEM) for o in outs])
    return outs[0], outs[1].T, outs[2].T, outs[3], outs[4].reshape(D)


def solution(mesh):
    return jax.shard_map(
        body,
        mesh=mesh,
        in_specs=(
            P(("dp", "tensor"), None),
            P("dp", "tensor"),
            P("dp", "tensor"),
            P(("dp", "tensor"), None),
            P(),
            P(None, "tensor"),
            P(None, "tensor"),
            P("tensor", None),
        ),
        out_specs=(
            P(("dp", "tensor"), None),
            P("dp", "tensor"),
            P("dp", "tensor"),
            P("tensor", "dp"),
            P(),
        ),
        check_vma=False,
    )
```

time: 134 us -> 117 us (0.87)
  Pallas kernels: 133 us -> 116 us
    pallas_call x1, Pallas kernels: 131 us -> 115 us  [body(): pl.pallas_call(kernel, out_shape=(V((32, D), BF), V((F, 256), BF), V((F,...]
where the time goes in v3:
time: 117 us
  Pallas kernels  116 us (99%)
    pallas_call x1, Pallas kernels, body(): pl.pallas_call(kernel, out_shape=(V((32, D), BF), V((F, 256), BF), V((F,...  115 us

profile of v3, /device:TPU:1, one launch (start us, length us, event | category | flops | bytes accessed | tf_op | source)
XLA Modules:
  0.0 117.1 jit_solution(3394938667514337111)
XLA Ops:
  0.6 115.5 %shard_map.119 = (bf16[32,4096]{1,0:T(8,128)(2,1)S(1)}, bf16[448,256]{1,0:T(8,128)(2,1)S(1)}, bf16[448,256]{1,0:T(8,128)(2,1)S(1)}, bf16[448,256]{1,0:T(8,128)(2,1)S(1)}, f32[1,4096]{1,0:T(1,128)S(1)}) custom-call(bf16[32,4096]{1,0:T(8,128)(2,1)} %inputs.1, bf16[448,512]{1,0:T(8,128)(2,1)} %bitcast.10, bf16[448,512]{1,0:T(8,128)(2,1)} %bitcast.11, ...), custom_call_target="tpu_custom_call" | custom-call | tf_op jit(solution)/shard_map/pallas_call | solution.py:600
  116.1 1.0 shard_map.120

commit v4 on v3

--- a/solution.py
+++ b/solution.py
@@ -17,53 +17,55 @@
 QW = D // NQ
 KS = (0, 1, 3, 2)
 MODES = {'G': 'zzzz', 'N': 'zzyz', 'R': 'zzzy'}
+RW = (5, 13, 6, 8)
 ORDER = (
-    ('G', 'e0', 0), ('G', 'e0', 2), ('G', 's2', 2, 0), ('G', 's2', 0, 0), ('G', 'e0', 1), ('G', 's2', 1, 0),
-    ('prefac',), ('normed',), ('hx',), ('nx',), ('N', 'e0', 2), ('G', 'e0', 3), ('G', 's2', 3, 0),
-    ('G', 'f2', 2, 0, 3), ('G', 'f2', 2, 0, 1), ('G', 'f1', 0, 3), ('G', 'f1', 0, 1), ('G', 's2', 0, 3),
-    ('G', 's2', 0, 1), ('G', 'f2', 0, 0, 3), ('G', 'f2', 0, 0, 1), ('G', 'f2', 1, 0, 3), ('G', 'f2', 1, 0, 1),
-    ('G', 'f1', 2, 3), ('G', 's2', 2, 3), ('G', 'f1', 2, 1), ('N', 'f1', 2, 3), ('N', 'f1', 2, 1),
-    ('G', 'f2', 3, 0, 3), ('G', 'f2', 3, 0, 1), ('G', 's2', 2, 1), ('G', 'f1', 1, 3), ('G', 'f1', 1, 1),
-    ('G', 'f2', 0, 3, 3), ('G', 'f2', 0, 3, 1), ('N', 'e0', 3), ('G', 's2', 1, 3), ('G', 'f2', 0, 1, 3),
-    ('G', 'f2', 0, 1, 1), ('G', 'f1', 3, 3), ('G', 'f1', 3, 1), ('G', 's2', 1, 1), ('G', 'e3', 0), ('G', 's2', 0, 2),
-    ('G', 'f2', 2, 3, 3), ('G', 'f2', 2, 3, 1), ('N', 'e0', 1), ('G', 'e3', 2), ('N', 'e3', 2), ('G', 'e3', 1),
-    ('G', 's2', 1, 2), ('G', 'f2', 2, 1, 3), ('G', 'f2', 2, 1, 1), ('N', 'e0', 0), ('G', 's2', 2, 2),
-    ('N', 'f1', 3, 3), ('N', 'f1', 3, 1), ('G', 'f2', 1, 3, 3), ('G', 'f2', 1, 3, 1), ('G', 'e3', 3),
-    ('G', 's2', 3, 3), ('G', 'f2', 1, 1, 3), ('G', 'f2', 1, 1, 1), ('N', 's2', 2, 0), ('G', 'f2', 0, 2, 3),
-    ('G', 'f2', 0, 2, 1), ('N', 'f1', 1, 3), ('N', 'f1', 1, 1), ('G', 's2', 3, 1), ('G', 'f2', 1, 2, 3),
-    ('G', 'f2', 1, 2, 1), ('G', 's2', 3, 2), ('N', 'f1', 0, 3), ('N', 'f1', 0, 1), ('G', 'f2', 2, 2, 3),
-    ('G', 'f2', 2, 2, 1), ('N', 's2', 2, 3), ('N', 'e3', 3), ('N', 's2', 0, 0), ('G', 'f2', 3, 3, 3),
-    ('G', 'f2', 3, 3, 1), ('N', 'f2', 2, 0, 3), ('N', 'f2', 2, 0, 1), ('N', 's2', 0, 3), ('G', 'done', 0), ('gh', 0),
-    ('N', 's2', 2, 1), ('N', 'e3', 1), ('N', 's2', 0, 1), ('G', 'f2', 3, 1, 3), ('G', 'f2', 3, 1, 1),
-    ('G', 'done', 1), ('gh', 1), ('dr', 0), ('D', 'part', 2), ('G', 'f2', 3, 2, 3), ('G', 'f2', 3, 2, 1), ('D', 'x2'),
-    ('G', 'done', 2), ('N', 's2', 1, 0), ('N', 'e3', 0), ('N', 's2', 2, 2), ('gh', 2), ('dr', 1), ('D', 'part', 1),
-    ('N', 's2', 0, 2), ('N', 'f2', 0, 0, 3), ('N', 'f2', 0, 0, 1), ('N', 'f2', 2, 3, 3), ('N', 'f2', 2, 3, 1),
-    ('dr', 2), ('D', 'part', 3), ('N', 'f2', 0, 3, 3), ('N', 'f2', 0, 3, 1), ('N', 's2', 1, 3), ('N', 'f2', 0, 1, 3),
-    ('N', 'f2', 0, 1, 1), ('N', 'f2', 2, 1, 3), ('N', 'f2', 2, 1, 1), ('N', 's2', 1, 1), ('G', 'done', 3), ('gh', 3),
-    ('acts',), ('tr',), ('pp', 6), ('D', 'x1'), ('D', 'x3'), ('pp', 7), ('N', 'f2', 0, 2, 3), ('N', 'f2', 0, 2, 1),
-    ('N', 's2', 1, 2), ('N', 'f2', 2, 2, 3), ('N', 'f2', 2, 2, 1), ('pp', 2), ('wready',), ('N', 'f2', 1, 0, 3),
-    ('N', 'f2', 1, 0, 1), ('pp', 1), ('N', 'f2', 1, 3, 3), ('N', 'f2', 1, 3, 1), ('R', 'r0', 3, 2), ('R', 'r0', 3, 1),
-    ('R', 'r0', 3, 3), ('R', 'r0', 3, 0), ('N', 's2', 3, 0), ('pp', 0), ('N', 's2', 3, 3), ('R', 'r0', 0, 2),
-    ('pp', 3), ('N', 'f2', 1, 1, 3), ('N', 'f2', 1, 1, 1), ('dr', 3), ('D', 'part', 0), ('N', 'done', 0),
-    ('W', 'part', 2), ('W', 'x2'), ('N', 'f2', 1, 2, 3), ('N', 'f2', 1, 2, 1), ('R', 'r1', 3, 2, 0),
-    ('R', 'r1', 3, 2, 1), ('N', 's2', 3, 1), ('N', 's2', 3, 2), ('N', 'done', 2), ('W', 'part', 3), ('W', 'x3i'),
-    ('N', 'f2', 3, 0, 3), ('N', 'f2', 3, 0, 1), ('R', 'r1', 3, 1, 0), ('R', 'r1', 3, 1, 1), ('R', 'r1', 3, 3, 0),
-    ('R', 'r1', 3, 3, 1), ('R', 'r0', 0, 1), ('N', 'f2', 3, 3, 3), ('N', 'f2', 3, 3, 1), ('R', 'r0', 0, 3), ('pp', 4),
-    ('R', 'r1', 3, 0, 0), ('R', 'r1', 3, 0, 1), ('R', 'r0', 0, 0), ('R', 'r0', 1, 2), ('R', 'r1', 0, 2, 0),
-    ('R', 'r1', 0, 2, 1), ('D', 'cross'), ('pp', 5), ('N', 'done', 1), ('W', 'part', 1), ('N', 'f2', 3, 1, 3),
-    ('N', 'f2', 3, 1, 1), ('R', 'r2', 3, 2), ('R', 'r0', 2, 2), ('W', 'x1i'), ('N', 'f2', 3, 2, 3),
-    ('N', 'f2', 3, 2, 1), ('R', 'r2', 3, 1), ('R', 'r0', 2, 1), ('R', 'r1', 0, 1, 0), ('R', 'r1', 0, 1, 1),
-    ('R', 'r1', 0, 3, 0), ('R', 'r1', 0, 3, 1), ('R', 'r1', 0, 0, 0), ('R', 'r1', 0, 0, 1), ('R', 'r2', 3, 3),
-    ('R', 'r1', 1, 2, 0), ('R', 'r1', 1, 2, 1), ('R', 'r2', 0, 2), ('W', 'x1d'), ('W', 'x3d'), ('R', 'r2', 3, 0),
-    ('R', 'r4', 3, 0), ('R', 'r4', 3, 1), ('R', 'r1', 2, 2, 0), ('R', 'r1', 2, 2, 1), ('N', 'done', 3),
-    ('W', 'part', 0), ('R', 'r0', 2, 3), ('R', 'r1', 2, 1, 0), ('R', 'r1', 2, 1, 1), ('R', 'r2', 0, 1), ('D', 'fin'),
-    ('R', 'r2', 0, 3), ('R', 'r0', 2, 0), ('R', 'r4', 0, 0), ('R', 'r4', 0, 1), ('R', 'r0', 1, 1), ('R', 'r2', 0, 0),
-    ('R', 'r0', 1, 3), ('R', 'r0', 1, 0), ('R', 'r2', 1, 2), ('R', 'r5', 3), ('W', 'cross'), ('R', 'r2', 2, 2),
-    ('R', 'r1', 2, 3, 0), ('R', 'r1', 2, 3, 1), ('R', 'r5', 0), ('R', 'r2', 2, 1), ('R', 'r1', 2, 0, 0),
-    ('R', 'r1', 2, 0, 1), ('R', 'r1', 1, 1, 0), ('R', 'r1', 1, 1, 1), ('R', 'r1', 1, 3, 0), ('R', 'r1', 1, 3, 1),
-    ('R', 'r1', 1, 0, 0), ('R', 'r1', 1, 0, 1), ('R', 'r2', 2, 3), ('R', 'r2', 2, 0), ('W', 'own'), ('R', 'r2', 1, 1),
-    ('R', 'r4', 1, 0), ('R', 'r2', 1, 3), ('R', 'r4', 1, 1), ('R', 'r2', 1, 0), ('W', 'fin'), ('R', 'r4', 2, 0),
-    ('R', 'r4', 2, 1), ('gain1',), ('R', 'r5', 1), ('R', 'r5', 2), ('fin',), ('gain2',),
+    ('G', 'e0', 0), ('G', 'e0', 3), ('G', 's2', 3, 0), ('G', 'e0', 1), ('G', 's2', 1, 0), ('G', 'e0', 2),
+    ('G', 's2', 2, 0), ('prefac',), ('normed',), ('G', 's2', 0, 0), ('hx',), ('nx',), ('N', 'e0', 2),
+    ('G', 'f2', 3, 0, 3), ('G', 'f2', 3, 0, 1), ('G', 'f1', 0, 3), ('G', 'f1', 0, 1), ('G', 's2', 0, 3),
+    ('G', 's2', 0, 1), ('G', 'f2', 1, 0, 3), ('G', 'f2', 1, 0, 1), ('G', 'f2', 2, 0, 3), ('G', 'f2', 2, 0, 1),
+    ('G', 'f1', 3, 3), ('G', 'f1', 3, 1), ('G', 'f2', 0, 0, 3), ('G', 'f2', 0, 0, 1), ('G', 's2', 3, 3),
+    ('N', 'f1', 2, 3), ('N', 'f1', 2, 1), ('G', 'f1', 1, 3), ('G', 'f1', 1, 1), ('G', 's2', 1, 3),
+    ('G', 'f2', 0, 3, 3), ('G', 'f2', 0, 3, 1), ('G', 'f2', 0, 1, 3), ('N', 'e0', 3), ('G', 'f2', 0, 1, 1),
+    ('G', 'f1', 2, 3), ('G', 'f1', 2, 1), ('G', 's2', 2, 3), ('G', 'e3', 0), ('G', 's2', 0, 2), ('G', 'e3', 3),
+    ('G', 'f2', 3, 3, 3), ('G', 'f2', 3, 3, 1), ('N', 'e0', 1), ('N', 'e3', 2), ('G', 's2', 2, 1), ('G', 'e3', 1),
+    ('G', 'f2', 1, 3, 3), ('G', 'f2', 1, 3, 1), ('G', 's2', 1, 1), ('N', 'e0', 0), ('N', 'f1', 3, 3),
+    ('N', 'f1', 3, 1), ('G', 's2', 1, 2), ('G', 'f2', 2, 3, 3), ('G', 'f2', 2, 3, 1), ('G', 'e3', 2),
+    ('G', 'f2', 0, 2, 3), ('G', 'f2', 0, 2, 1), ('G', 's2', 2, 2), ('N', 's2', 2, 0), ('N', 'f1', 1, 3),
+    ('N', 'f1', 1, 1), ('G', 'f2', 2, 1, 3), ('G', 'f2', 2, 1, 1), ('G', 's2', 3, 1), ('G', 'f2', 1, 1, 3),
+    ('G', 'f2', 1, 1, 1), ('N', 'f1', 0, 3), ('N', 'f1', 0, 1), ('G', 's2', 3, 2), ('G', 'f2', 1, 2, 3),
+    ('G', 'f2', 1, 2, 1), ('N', 'e3', 3), ('N', 's2', 2, 3), ('G', 'done', 0), ('gh', 0), ('N', 's2', 0, 0),
+    ('G', 'f2', 2, 2, 3), ('G', 'f2', 2, 2, 1), ('N', 'f2', 2, 0, 3), ('N', 'f2', 2, 0, 1), ('dr', 0),
+    ('D', 'part', 2), ('G', 'f2', 3, 1, 3), ('G', 'f2', 3, 1, 1), ('D', 'x2'), ('N', 's2', 0, 3), ('N', 'e3', 1),
+    ('N', 's2', 2, 1), ('N', 'e3', 0), ('N', 's2', 0, 1), ('G', 'f2', 3, 2, 3), ('G', 'f2', 3, 2, 1),
+    ('G', 'done', 1), ('gh', 1), ('N', 's2', 2, 2), ('N', 's2', 0, 2), ('N', 'f2', 2, 3, 3), ('N', 'f2', 2, 3, 1),
+    ('N', 'f2', 0, 0, 3), ('N', 'f2', 0, 0, 1), ('G', 'done', 2), ('gh', 2), ('dr', 1), ('D', 'part', 1),
+    ('N', 's2', 1, 0), ('N', 'f2', 0, 3, 3), ('N', 'f2', 0, 3, 1), ('dr', 2), ('D', 'part', 3), ('D', 'x1'),
+    ('D', 'x3'), ('N', 'f2', 2, 1, 3), ('G', 'done', 3), ('N', 'f2', 2, 1, 1), ('N', 's2', 1, 3), ('gh', 3),
+    ('N', 's2', 1, 1), ('acts',), ('N', 'f2', 0, 1, 3), ('N', 'f2', 0, 1, 1), ('N', 'f2', 0, 2, 3),
+    ('N', 'f2', 0, 2, 1), ('tr',), ('pp', 6), ('N', 'f2', 2, 2, 3), ('N', 'f2', 2, 2, 1), ('pp', 2),
+    ('N', 's2', 1, 2), ('N', 'f2', 1, 0, 3), ('N', 'f2', 1, 0, 1), ('pp', 7), ('wready',), ('R', 'r0', 3, 2),
+    ('R', 'r0', 3, 1), ('R', 'r0', 3, 3), ('R', 'r0', 3, 0), ('pp', 4), ('N', 's2', 3, 0), ('N', 'f2', 1, 3, 3),
+    ('N', 'f2', 1, 3, 1), ('pp', 1), ('pp', 0), ('N', 's2', 3, 3), ('N', 'f2', 1, 1, 3), ('N', 'f2', 1, 1, 1),
+    ('R', 'r0', 0, 2), ('pp', 3), ('N', 'done', 0), ('W', 'part', 2), ('N', 's2', 3, 1), ('R', 'r1', 3, 2, 0),
+    ('N', 's2', 3, 2), ('R', 'r1', 3, 2, 1), ('R', 'r1', 3, 1, 0), ('R', 'r1', 3, 1, 1), ('R', 'r1', 3, 3, 0),
+    ('R', 'r1', 3, 3, 1), ('N', 'f2', 1, 2, 3), ('N', 'f2', 1, 2, 1), ('R', 'r0', 0, 1), ('R', 'r0', 0, 3),
+    ('W', 'x2'), ('dr', 3), ('D', 'part', 0), ('D', 'cross'), ('R', 'r1', 3, 0, 0), ('R', 'r1', 3, 0, 1),
+    ('R', 'r0', 0, 0), ('R', 'r0', 1, 2), ('pp', 5), ('R', 'r0', 2, 2), ('R', 'r0', 2, 1), ('N', 'f2', 3, 0, 3),
+    ('N', 'f2', 3, 0, 1), ('N', 'f2', 3, 3, 3), ('N', 'f2', 3, 3, 1), ('N', 'done', 2), ('R', 'r1', 0, 2, 0),
+    ('R', 'r1', 0, 2, 1), ('W', 'part', 3), ('R', 'r0', 2, 3), ('W', 'x3i'), ('N', 'f2', 3, 1, 3),
+    ('N', 'f2', 3, 1, 1), ('N', 'f2', 3, 2, 3), ('N', 'f2', 3, 2, 1), ('R', 'r2', 3, 2), ('N', 'done', 1),
+    ('W', 'part', 1), ('R', 'r1', 1, 2, 0), ('R', 'r1', 1, 2, 1), ('R', 'r1', 0, 1, 0), ('R', 'r1', 0, 1, 1),
+    ('R', 'r1', 0, 3, 0), ('R', 'r1', 2, 2, 0), ('R', 'r1', 2, 2, 1), ('R', 'r1', 0, 3, 1), ('R', 'r1', 0, 0, 0),
+    ('R', 'r1', 2, 1, 0), ('R', 'r1', 2, 1, 1), ('R', 'r1', 0, 0, 1), ('W', 'x1i'), ('R', 'r2', 3, 1),
+    ('R', 'r2', 3, 3), ('R', 'r2', 0, 2), ('W', 'x1d'), ('R', 'r1', 2, 3, 0), ('R', 'r1', 2, 3, 1), ('W', 'x3d'),
+    ('N', 'done', 3), ('W', 'part', 0), ('D', 'fin'), ('R', 'r0', 2, 0), ('R', 'r0', 1, 1), ('R', 'r4', 3, 0),
+    ('R', 'r2', 1, 2), ('R', 'r4', 3, 1), ('gain0',), ('R', 'r2', 0, 1), ('R', 'r2', 3, 0), ('R', 'r4', 0, 0),
+    ('R', 'r0', 1, 3), ('R', 'r2', 2, 2), ('R', 'r2', 0, 3), ('R', 'r4', 0, 1), ('R', 'r0', 1, 0), ('R', 'r2', 2, 1),
+    ('R', 'r2', 0, 0), ('W', 'cross'), ('R', 'r2', 2, 3), ('R', 'r1', 2, 0, 0), ('R', 'r1', 2, 0, 1),
+    ('R', 'r4', 2, 1), ('R', 'r1', 1, 1, 0), ('R', 'r1', 1, 1, 1), ('R', 'r5', 0), ('R', 'r4', 2, 0), ('R', 'r5', 3),
+    ('R', 'r1', 1, 3, 1), ('R', 'r1', 1, 3, 0), ('R', 'r1', 1, 0, 1), ('R', 'r1', 1, 0, 0), ('R', 'r2', 2, 0),
+    ('gain1',), ('R', 'r2', 1, 1), ('R', 'r4', 1, 0), ('R', 'r2', 1, 3), ('R', 'r4', 1, 1), ('W', 'fin'),
+    ('R', 'r2', 1, 0), ('R', 'r5', 2), ('gain2',), ('R', 'r5', 1), ('fin',),
 )
 RELS = (2, 1, 3, 0)
 
@@ -380,14 +382,19 @@
         def part(self, rel):
             xr = ring(x, rel)
 
-            @pl.loop(0, 4)
-            def _(i):
-                z, k = i // 2, lax.rem(i, 2)
-                cols = pl.ds(pl.multiple_of((xr * 2 + z) * 256, 256), 256)
+            @pl.loop(0, 2)
+            def _(z):
+                j = xr * 2 + z
+                cols = pl.ds(pl.multiple_of(j * 256, 256), 256)
+                wcols = pl.ds(pl.multiple_of((2 * j + c) * 256, 256), 256)
                 mine = n_all[c, :, :, cols].reshape(T, 256)
                 his = n_all[oc, :, :, cols].reshape(T, 256)
-                v = dot_nn(act_t[1 + k], mine) + dot_nn(act_s[1 + k], his)
-                xp_w[xr, k, z] = v.astype(BF)
+                gsum = jnp.zeros((8, 256), F32)
+                for k, w_ref in enumerate((wg, wu)):
+                    v = dot_nn(act_t[1 + k], mine) + dot_nn(act_s[1 + k], his)
+                    xp_w[xr, k, z] = v.astype(BF)
+                    gsum = gsum + jnp.sum((v * w_ref[:, wcols].astype(F32)).reshape(F // 8, 8, 256), axis=0)
+                gt[t, pl.ds(j, 1), :] = jnp.sum(gsum, axis=0, keepdims=True) / vgain[:, wcols]
 
         def x2(self):
             xr = ring(x, 2)
@@ -418,46 +425,32 @@
             add_rows(xp_w.at[xr, 1, zl], [xh_w.at[1, zl]], F, 64)
             self.push(xp_w.at[xr, 1, zl], xf_w.at[1, 1, zl], 7, xdev(3))
 
-        def gather_sum(self, z):
-            cols = pl.ds(pl.multiple_of((x * 4 + z * 2 + c) * 256, 256), 256)
-            gsum = jnp.zeros((8, 256), F32)
-            for k, w_ref in enumerate((wg, wu)):
-                def step(r, acc):
-                    rr = pl.ds(pl.multiple_of(r * 64, 64), 64)
-                    v = xp_w[x, k, z, rr, :].astype(F32) + xf_w[0, k, z, rr, :].astype(F32)
-                    v = v + xf_w[1, k, z, rr, :].astype(F32)
-                    xp_w[x, k, z, rr, :] = v.astype(BF)
-                    return acc + jnp.sum((v * w_ref[rr, cols].astype(F32)).reshape(8, 8, 256), axis=0)
-
-                gsum = lax.fori_loop(0, F // 64, step, gsum)
-            gt[t, pl.ds(z, 1), :] = jnp.sum(gsum, axis=0, keepdims=True) / vgain[:, cols]
-
         def cross(self):
             self.get(xf_w.at[0, 1, oz], 2, xdev(3))
             self.get(xf_w.at[1, 0, oz], 3, xdev(1))
             self.get(xf_w.at[0, 0, oz], 4, xdev(3))
             self.get(xf_w.at[1, 1, oz], 6, xdev(1))
-            gt[t] = jnp.zeros((8, 256), F32)
-            self.gather_sum(oz)
+            for k in (0, 1):
+                add_rows(xp_w.at[x, k, oz], [xf_w.at[0, k, oz], xf_w.at[1, k, oz]], F, 64)
             self.push(xp_w.at[x, :, oz], xz_w, 8, zsib)
 
-        def own(self):
+        def fin(self):
             self.get(xf_w.at[0, 1, zl], 9, xdev(3))
             self.get(xf_w.at[1, 0, zl], 10, xdev(1))
             self.get(xf_w.at[0, 0, zl], 5, xdev(3))
             self.get(xf_w.at[1, 1, zl], 7, xdev(1))
-            self.gather_sum(zl)
-            for k in range(1, 16):
-                send(gt.at[t], gt.at[t], g_s.at[0], g_r.at[0], tdev(k))
-
-        def fin(self):
             self.get(xz_w, 8, zsib)
             for k, o_ref in enumerate((o_gate, o_up)):
                 @pl.loop(0, F // 64)
                 def _(r):
                     rr = pl.ds(pl.multiple_of(r * 64, 64), 64)
-                    o_ref[rr, :] = (xp_w[x, k, zl, rr, :].astype(F32) + xz_w[k, rr, :].astype(F32)).astype(BF)
-
+                    v = xp_w[x, k, zl, rr, :].astype(F32) + xf_w[0, k, zl, rr, :].astype(F32)
+                    v = v + xf_w[1, k, zl, rr, :].astype(F32) + xz_w[k, rr, :].astype(F32)
+                    o_ref[rr, :] = v.astype(BF)
+
+    def gain0():
+        for k in range(1, 16):
+            send(gt.at[t], gt.at[t], g_s.at[0], g_r.at[0], tdev(k))
 
     def gain1():
         recv(gt.at[pl.ds(0, 15)], g_r.at[0], g_s.at[0], tdev(1))
@@ -467,9 +460,12 @@
 
     def gain2():
         recv(og.at[pl.ds(0, 15)], g_r.at[1], g_s.at[1], pdev(1))
-        for k in range(16):
-            z, k0 = (k // 2) % 2, k - k % 4 + k % 2
-            o_gain[:, pl.ds(k * 256, 256)] = og[k0, z : z + 1, :] + og[k0 + 2, z : z + 1, :]
+        for k in (0, 1):
+            v = og[k]
+            for i in range(1, 8):
+                v = v + og[2 * i + k]
+            for j in range(8):
+                o_gain[:, pl.ds((2 * j + k) * 256, 256)] = v[j : j + 1, :]
 
     def p_part(i):
         if "pp" not in begun:
@@ -482,7 +478,7 @@
 
     class Scatter:
         def __init__(self, q, zlast):
-            self.cols = pl.ds(q * QW, QW)
+            self.cols = pl.ds(128 * sum(RW[:q]), 128 * RW[q])
             self.zlast = zlast
             self.dev1 = ydev if zlast else zdev
             self.dev2 = zdev if zlast else ydev
@@ -563,7 +559,7 @@
     whole = {"D": DownSum(), "W": WeightSum()}
     single = {
         "normed": normed, "nx": nx, "prefac": prefac, "gh": gh_add, "acts": act_grads, "tr": turn, "hx": h_ready, "dr": d_ready,
-        "wready": w_ready, "pp": p_part, "gain1": gain1, "gain2": gain2, "fin": finish,
+        "wready": w_ready, "pp": p_part, "gain0": gain0, "gain1": gain1, "gain2": gain2, "fin": finish,
     }
     for name, *rest in ORDER:
         if name in per_quarter:

time: 117 us -> 115 us (0.983)
  Pallas kernels: 116 us -> 114 us
    pallas_call x1, Pallas kernels: 115 us -> 113 us  [body(): pl.pallas_call(kernel, out_shape=(V((32, D), BF), V((F, 256), BF), V((F,...]
where the time goes in v4:
time: 115 us
  Pallas kernels  114 us (99%)
    pallas_call x1, Pallas kernels, body(): pl.pallas_call(kernel, out_shape=(V((32, D), BF), V((F, 256), BF), V((F,...  113 us

profile of v4, /device:TPU:1, one launch (start us, length us, event | category | flops | bytes accessed | tf_op | source)
XLA Modules:
  0.0 114.7 jit_solution(14123992132536941728)
XLA Ops:
  0.6 113.1 %shard_map.119 = (bf16[32,4096]{1,0:T(8,128)(2,1)S(1)}, bf16[448,256]{1,0:T(8,128)(2,1)S(1)}, bf16[448,256]{1,0:T(8,128)(2,1)S(1)}, bf16[448,256]{1,0:T(8,128)(2,1)S(1)}, f32[1,4096]{1,0:T(1,128)S(1)}) custom-call(bf16[32,4096]{1,0:T(8,128)(2,1)} %inputs.1, bf16[448,512]{1,0:T(8,128)(2,1)} %bitcast.10, bf16[448,512]{1,0:T(8,128)(2,1)} %bitcast.11, ...), custom_call_target="tpu_custom_call" | custom-call | tf_op jit(solution)/shard_map/pallas_call | solution.py:596
  113.8 1.0 shard_map.120

commit v5 on v4

--- a/solution.py
+++ b/solution.py
@@ -17,55 +17,55 @@
 QW = D // NQ
 KS = (0, 1, 3, 2)
 MODES = {'G': 'zzzz', 'N': 'zzyz', 'R': 'zzzy'}
-RW = (5, 13, 6, 8)
+RW = (9, 10, 6, 7)
 ORDER = (
-    ('G', 'e0', 0), ('G', 'e0', 3), ('G', 's2', 3, 0), ('G', 'e0', 1), ('G', 's2', 1, 0), ('G', 'e0', 2),
-    ('G', 's2', 2, 0), ('prefac',), ('normed',), ('G', 's2', 0, 0), ('hx',), ('nx',), ('N', 'e0', 2),
-    ('G', 'f2', 3, 0, 3), ('G', 'f2', 3, 0, 1), ('G', 'f1', 0, 3), ('G', 'f1', 0, 1), ('G', 's2', 0, 3),
-    ('G', 's2', 0, 1), ('G', 'f2', 1, 0, 3), ('G', 'f2', 1, 0, 1), ('G', 'f2', 2, 0, 3), ('G', 'f2', 2, 0, 1),
-    ('G', 'f1', 3, 3), ('G', 'f1', 3, 1), ('G', 'f2', 0, 0, 3), ('G', 'f2', 0, 0, 1), ('G', 's2', 3, 3),
+    ('G', 'e0', 0), ('G', 'e0', 3), ('G', 'e0', 1), ('G', 's2', 1, 0), ('G', 's2', 3, 0), ('prefac',), ('normed',),
+    ('G', 's2', 0, 0), ('G', 'e0', 2), ('G', 's2', 2, 0), ('nx',), ('N', 'e0', 2), ('G', 'f2', 1, 0, 3),
+    ('G', 'f2', 1, 0, 1), ('G', 'f1', 0, 3), ('G', 'f1', 0, 1), ('G', 's2', 0, 3), ('G', 's2', 0, 1),
+    ('G', 'f2', 3, 0, 3), ('G', 'f2', 3, 0, 1), ('hx',), ('G', 'f2', 0, 0, 3), ('G', 'f2', 0, 0, 1),
+    ('G', 'f1', 3, 3), ('G', 'f1', 3, 1), ('G', 'f2', 2, 0, 3), ('G', 'f2', 2, 0, 1), ('G', 's2', 3, 3),
     ('N', 'f1', 2, 3), ('N', 'f1', 2, 1), ('G', 'f1', 1, 3), ('G', 'f1', 1, 1), ('G', 's2', 1, 3),
-    ('G', 'f2', 0, 3, 3), ('G', 'f2', 0, 3, 1), ('G', 'f2', 0, 1, 3), ('N', 'e0', 3), ('G', 'f2', 0, 1, 1),
+    ('G', 'f2', 0, 3, 3), ('G', 'f2', 0, 3, 1), ('G', 'f2', 0, 1, 3), ('G', 'f2', 0, 1, 1), ('N', 'e0', 3),
     ('G', 'f1', 2, 3), ('G', 'f1', 2, 1), ('G', 's2', 2, 3), ('G', 'e3', 0), ('G', 's2', 0, 2), ('G', 'e3', 3),
-    ('G', 'f2', 3, 3, 3), ('G', 'f2', 3, 3, 1), ('N', 'e0', 1), ('N', 'e3', 2), ('G', 's2', 2, 1), ('G', 'e3', 1),
-    ('G', 'f2', 1, 3, 3), ('G', 'f2', 1, 3, 1), ('G', 's2', 1, 1), ('N', 'e0', 0), ('N', 'f1', 3, 3),
+    ('G', 'f2', 3, 3, 3), ('G', 'f2', 3, 3, 1), ('N', 'e3', 2), ('N', 'e0', 0), ('G', 'e3', 1), ('G', 's2', 2, 1),
+    ('G', 'f2', 1, 3, 3), ('G', 'f2', 1, 3, 1), ('G', 's2', 1, 1), ('N', 'e0', 1), ('N', 'f1', 3, 3),
     ('N', 'f1', 3, 1), ('G', 's2', 1, 2), ('G', 'f2', 2, 3, 3), ('G', 'f2', 2, 3, 1), ('G', 'e3', 2),
-    ('G', 'f2', 0, 2, 3), ('G', 'f2', 0, 2, 1), ('G', 's2', 2, 2), ('N', 's2', 2, 0), ('N', 'f1', 1, 3),
-    ('N', 'f1', 1, 1), ('G', 'f2', 2, 1, 3), ('G', 'f2', 2, 1, 1), ('G', 's2', 3, 1), ('G', 'f2', 1, 1, 3),
-    ('G', 'f2', 1, 1, 1), ('N', 'f1', 0, 3), ('N', 'f1', 0, 1), ('G', 's2', 3, 2), ('G', 'f2', 1, 2, 3),
-    ('G', 'f2', 1, 2, 1), ('N', 'e3', 3), ('N', 's2', 2, 3), ('G', 'done', 0), ('gh', 0), ('N', 's2', 0, 0),
-    ('G', 'f2', 2, 2, 3), ('G', 'f2', 2, 2, 1), ('N', 'f2', 2, 0, 3), ('N', 'f2', 2, 0, 1), ('dr', 0),
-    ('D', 'part', 2), ('G', 'f2', 3, 1, 3), ('G', 'f2', 3, 1, 1), ('D', 'x2'), ('N', 's2', 0, 3), ('N', 'e3', 1),
-    ('N', 's2', 2, 1), ('N', 'e3', 0), ('N', 's2', 0, 1), ('G', 'f2', 3, 2, 3), ('G', 'f2', 3, 2, 1),
-    ('G', 'done', 1), ('gh', 1), ('N', 's2', 2, 2), ('N', 's2', 0, 2), ('N', 'f2', 2, 3, 3), ('N', 'f2', 2, 3, 1),
-    ('N', 'f2', 0, 0, 3), ('N', 'f2', 0, 0, 1), ('G', 'done', 2), ('gh', 2), ('dr', 1), ('D', 'part', 1),
-    ('N', 's2', 1, 0), ('N', 'f2', 0, 3, 3), ('N', 'f2', 0, 3, 1), ('dr', 2), ('D', 'part', 3), ('D', 'x1'),
-    ('D', 'x3'), ('N', 'f2', 2, 1, 3), ('G', 'done', 3), ('N', 'f2', 2, 1, 1), ('N', 's2', 1, 3), ('gh', 3),
-    ('N', 's2', 1, 1), ('acts',), ('N', 'f2', 0, 1, 3), ('N', 'f2', 0, 1, 1), ('N', 'f2', 0, 2, 3),
-    ('N', 'f2', 0, 2, 1), ('tr',), ('pp', 6), ('N', 'f2', 2, 2, 3), ('N', 'f2', 2, 2, 1), ('pp', 2),
-    ('N', 's2', 1, 2), ('N', 'f2', 1, 0, 3), ('N', 'f2', 1, 0, 1), ('pp', 7), ('wready',), ('R', 'r0', 3, 2),
-    ('R', 'r0', 3, 1), ('R', 'r0', 3, 3), ('R', 'r0', 3, 0), ('pp', 4), ('N', 's2', 3, 0), ('N', 'f2', 1, 3, 3),
-    ('N', 'f2', 1, 3, 1), ('pp', 1), ('pp', 0), ('N', 's2', 3, 3), ('N', 'f2', 1, 1, 3), ('N', 'f2', 1, 1, 1),
-    ('R', 'r0', 0, 2), ('pp', 3), ('N', 'done', 0), ('W', 'part', 2), ('N', 's2', 3, 1), ('R', 'r1', 3, 2, 0),
-    ('N', 's2', 3, 2), ('R', 'r1', 3, 2, 1), ('R', 'r1', 3, 1, 0), ('R', 'r1', 3, 1, 1), ('R', 'r1', 3, 3, 0),
-    ('R', 'r1', 3, 3, 1), ('N', 'f2', 1, 2, 3), ('N', 'f2', 1, 2, 1), ('R', 'r0', 0, 1), ('R', 'r0', 0, 3),
-    ('W', 'x2'), ('dr', 3), ('D', 'part', 0), ('D', 'cross'), ('R', 'r1', 3, 0, 0), ('R', 'r1', 3, 0, 1),
-    ('R', 'r0', 0, 0), ('R', 'r0', 1, 2), ('pp', 5), ('R', 'r0', 2, 2), ('R', 'r0', 2, 1), ('N', 'f2', 3, 0, 3),
-    ('N', 'f2', 3, 0, 1), ('N', 'f2', 3, 3, 3), ('N', 'f2', 3, 3, 1), ('N', 'done', 2), ('R', 'r1', 0, 2, 0),
-    ('R', 'r1', 0, 2, 1), ('W', 'part', 3), ('R', 'r0', 2, 3), ('W', 'x3i'), ('N', 'f2', 3, 1, 3),
+    ('G', 'f2', 0, 2, 3), ('G', 'f2', 0, 2, 1), ('G', 's2', 2, 2), ('N', 's2', 2, 0), ('N', 'f1', 0, 3),
+    ('N', 'f1', 0, 1), ('G', 'f2', 2, 1, 3), ('G', 'f2', 2, 1, 1), ('G', 's2', 3, 1), ('G', 'f2', 1, 1, 3),
+    ('G', 'f2', 1, 1, 1), ('N', 'f1', 1, 3), ('N', 'f1', 1, 1), ('G', 's2', 3, 2), ('G', 'f2', 1, 2, 3),
+    ('G', 'f2', 1, 2, 1), ('N', 'e3', 3), ('G', 'done', 0), ('gh', 0), ('N', 's2', 0, 0), ('N', 's2', 2, 3),
+    ('G', 'f2', 2, 2, 3), ('G', 'f2', 2, 2, 1), ('N', 'f2', 2, 0, 3), ('N', 'f2', 2, 0, 1), ('N', 's2', 0, 3),
+    ('dr', 0), ('D', 'part', 2), ('D', 'x2'), ('G', 'f2', 3, 1, 3), ('G', 'f2', 3, 1, 1), ('N', 'e3', 0),
+    ('N', 's2', 2, 1), ('N', 'e3', 1), ('N', 's2', 0, 1), ('G', 'f2', 3, 2, 3), ('G', 'f2', 3, 2, 1),
+    ('G', 'done', 1), ('gh', 1), ('N', 's2', 0, 2), ('N', 's2', 2, 2), ('N', 'f2', 2, 3, 3), ('N', 'f2', 2, 3, 1),
+    ('N', 'f2', 0, 0, 3), ('N', 'f2', 0, 0, 1), ('G', 'done', 2), ('gh', 2), ('N', 's2', 1, 0), ('dr', 1),
+    ('D', 'part', 1), ('N', 'f2', 0, 3, 3), ('N', 'f2', 0, 3, 1), ('D', 'x1'), ('dr', 2), ('D', 'part', 3),
+    ('N', 'f2', 2, 1, 3), ('N', 'f2', 2, 1, 1), ('D', 'x3'), ('N', 's2', 1, 3), ('G', 'done', 3), ('N', 's2', 1, 1),
+    ('N', 'f2', 0, 1, 3), ('N', 'f2', 0, 1, 1), ('gh', 3), ('acts',), ('N', 'f2', 0, 2, 3), ('N', 'f2', 0, 2, 1),
+    ('tr',), ('N', 'f2', 2, 2, 3), ('N', 'f2', 2, 2, 1), ('pp', 2), ('pp', 6), ('pp', 7), ('wready',),
+    ('R', 'r0', 3, 2), ('R', 'r0', 3, 1), ('pp', 1), ('N', 's2', 1, 2), ('R', 'r0', 3, 3), ('N', 's2', 3, 0),
+    ('N', 's2', 3, 3), ('pp', 4), ('N', 'f2', 1, 0, 3), ('N', 'f2', 1, 0, 1), ('N', 'f2', 1, 3, 3),
+    ('N', 'f2', 1, 3, 1), ('R', 'r0', 3, 0), ('dr', 3), ('D', 'part', 0), ('N', 'f2', 1, 1, 3), ('N', 'f2', 1, 1, 1),
+    ('pp', 3), ('N', 'done', 0), ('W', 'part', 2), ('W', 'x2'), ('N', 's2', 3, 1), ('N', 's2', 3, 2),
+    ('N', 'f2', 1, 2, 3), ('N', 'f2', 1, 2, 1), ('R', 'r1', 3, 2, 0), ('R', 'r1', 3, 2, 1), ('R', 'r1', 3, 1, 0),
+    ('R', 'r1', 3, 1, 1), ('R', 'r1', 3, 3, 0), ('R', 'r1', 3, 3, 1), ('D', 'cross'), ('R', 'r0', 1, 2),
+    ('R', 'r1', 3, 0, 0), ('R', 'r1', 3, 0, 1), ('pp', 0), ('R', 'r0', 0, 2), ('pp', 5), ('R', 'r0', 2, 2),
+    ('N', 'f2', 3, 0, 3), ('N', 'f2', 3, 0, 1), ('N', 'f2', 3, 3, 3), ('N', 'f2', 3, 3, 1), ('N', 'done', 2),
+    ('W', 'part', 3), ('R', 'r0', 2, 1), ('R', 'r0', 2, 3), ('R', 'r0', 2, 0), ('W', 'x3i'), ('N', 'f2', 3, 1, 3),
     ('N', 'f2', 3, 1, 1), ('N', 'f2', 3, 2, 3), ('N', 'f2', 3, 2, 1), ('R', 'r2', 3, 2), ('N', 'done', 1),
-    ('W', 'part', 1), ('R', 'r1', 1, 2, 0), ('R', 'r1', 1, 2, 1), ('R', 'r1', 0, 1, 0), ('R', 'r1', 0, 1, 1),
-    ('R', 'r1', 0, 3, 0), ('R', 'r1', 2, 2, 0), ('R', 'r1', 2, 2, 1), ('R', 'r1', 0, 3, 1), ('R', 'r1', 0, 0, 0),
-    ('R', 'r1', 2, 1, 0), ('R', 'r1', 2, 1, 1), ('R', 'r1', 0, 0, 1), ('W', 'x1i'), ('R', 'r2', 3, 1),
-    ('R', 'r2', 3, 3), ('R', 'r2', 0, 2), ('W', 'x1d'), ('R', 'r1', 2, 3, 0), ('R', 'r1', 2, 3, 1), ('W', 'x3d'),
-    ('N', 'done', 3), ('W', 'part', 0), ('D', 'fin'), ('R', 'r0', 2, 0), ('R', 'r0', 1, 1), ('R', 'r4', 3, 0),
-    ('R', 'r2', 1, 2), ('R', 'r4', 3, 1), ('gain0',), ('R', 'r2', 0, 1), ('R', 'r2', 3, 0), ('R', 'r4', 0, 0),
-    ('R', 'r0', 1, 3), ('R', 'r2', 2, 2), ('R', 'r2', 0, 3), ('R', 'r4', 0, 1), ('R', 'r0', 1, 0), ('R', 'r2', 2, 1),
-    ('R', 'r2', 0, 0), ('W', 'cross'), ('R', 'r2', 2, 3), ('R', 'r1', 2, 0, 0), ('R', 'r1', 2, 0, 1),
-    ('R', 'r4', 2, 1), ('R', 'r1', 1, 1, 0), ('R', 'r1', 1, 1, 1), ('R', 'r5', 0), ('R', 'r4', 2, 0), ('R', 'r5', 3),
-    ('R', 'r1', 1, 3, 1), ('R', 'r1', 1, 3, 0), ('R', 'r1', 1, 0, 1), ('R', 'r1', 1, 0, 0), ('R', 'r2', 2, 0),
-    ('gain1',), ('R', 'r2', 1, 1), ('R', 'r4', 1, 0), ('R', 'r2', 1, 3), ('R', 'r4', 1, 1), ('W', 'fin'),
-    ('R', 'r2', 1, 0), ('R', 'r5', 2), ('gain2',), ('R', 'r5', 1), ('fin',),
+    ('W', 'part', 1), ('R', 'r1', 2, 2, 0), ('R', 'r1', 2, 2, 1), ('R', 'r1', 0, 2, 0), ('R', 'r1', 0, 2, 1),
+    ('R', 'r1', 1, 2, 0), ('R', 'r1', 1, 2, 1), ('W', 'x1i'), ('R', 'r2', 3, 1), ('R', 'r2', 3, 3),
+    ('R', 'r1', 2, 1, 0), ('R', 'r1', 2, 1, 1), ('R', 'r1', 2, 3, 0), ('R', 'r1', 2, 3, 1), ('R', 'r1', 2, 0, 0),
+    ('R', 'r1', 2, 0, 1), ('W', 'x3d'), ('W', 'x1d'), ('N', 'done', 3), ('W', 'part', 0), ('D', 'fin'),
+    ('R', 'r2', 2, 2), ('R', 'r0', 0, 1), ('gain0',), ('R', 'r2', 0, 2), ('R', 'r0', 0, 3), ('R', 'r4', 3, 0),
+    ('R', 'r4', 3, 1), ('R', 'r2', 3, 0), ('R', 'r2', 1, 2), ('R', 'r0', 0, 0), ('R', 'r2', 2, 1), ('R', 'r0', 1, 1),
+    ('R', 'r4', 2, 0), ('R', 'r2', 2, 3), ('R', 'r4', 2, 1), ('R', 'r0', 1, 3), ('R', 'r0', 1, 0), ('R', 'r2', 2, 0),
+    ('W', 'cross'), ('R', 'r1', 0, 1, 0), ('R', 'r1', 0, 1, 1), ('R', 'r1', 0, 3, 1), ('R', 'r1', 0, 3, 0),
+    ('R', 'r5', 3), ('R', 'r1', 0, 0, 1), ('R', 'r1', 0, 0, 0), ('R', 'r5', 2), ('R', 'r1', 1, 1, 1), ('gain1',),
+    ('R', 'r1', 1, 1, 0), ('R', 'r1', 1, 3, 0), ('R', 'r1', 1, 3, 1), ('R', 'r1', 1, 0, 1), ('R', 'r1', 1, 0, 0),
+    ('R', 'r2', 0, 1), ('R', 'r4', 0, 0), ('R', 'r2', 0, 3), ('R', 'r4', 0, 1), ('R', 'r2', 0, 0), ('R', 'r2', 1, 1),
+    ('R', 'r4', 1, 0), ('R', 'r2', 1, 3), ('R', 'r4', 1, 1), ('W', 'fin'), ('R', 'r2', 1, 0), ('gain2',),
+    ('R', 'r5', 0), ('R', 'r5', 1), ('fin',),
 )
 RELS = (2, 1, 3, 0)
 
@@ -149,18 +149,6 @@
         cp.start()
         local.append(cp)
 
-    local[0].wait()
-    local[1].wait()
-    xin = vin[...].astype(F32)
-    inv = lax.rsqrt(jnp.mean(xin * xin, axis=1, keepdims=True) + 1e-05)
-
-    @pl.loop(0, 8)
-    def _(j):
-        own = pl.ds(pl.multiple_of((2 * j + c) * 256, 256), 256)
-        oth = pl.ds(pl.multiple_of((2 * j + oc) * 256, 256), 256)
-        col = pl.ds(pl.multiple_of(j * 256, 256), 256)
-        n_all[c, t, :, col] = (vin[:, own].astype(F32) * inv * vgain[:, own]).astype(BF)
-        n_send[:, col] = (vin[:, oth].astype(F32) * inv * vgain[:, oth]).astype(BF)
     pl.semaphore_wait(barrier, len(partners))
 
     class Gather:
@@ -245,6 +233,19 @@
     ]
 
     def normed():
+        local[0].wait()
+        local[1].wait()
+        xin = vin[...].astype(F32)
+        inv = lax.rsqrt(jnp.mean(xin * xin, axis=1, keepdims=True) + 1e-05)
+
+        @pl.loop(0, 8)
+        def _(j):
+            own = pl.ds(pl.multiple_of((2 * j + c) * 256, 256), 256)
+            oth = pl.ds(pl.multiple_of((2 * j + oc) * 256, 256), 256)
+            col = pl.ds(pl.multiple_of(j * 256, 256), 256)
+            n_all[c, t, :, col] = (vin[:, own].astype(F32) * inv * vgain[:, own]).astype(BF)
+            n_send[:, col] = (vin[:, oth].astype(F32) * inv * vgain[:, oth]).astype(BF)
+
         sent.append(send(n_send, n_all.at[c, t], c_s.at[0], c_r.at[0], sib))
 
     def nx():

time: 115 us -> 113 us (0.983)
    pallas_call x1, Pallas kernels: 113 us -> 112 us  [body(): pl.pallas_call(kernel, out_shape=(V((32, D), BF), V((F, 256), BF), V((F,...]
where the time goes in v5:
time: 113 us
  Pallas kernels  113 us (100%)
    pallas_call x1, Pallas kernels, body(): pl.pallas_call(kernel, out_shape=(V((32, D), BF), V((F, 256), BF), V((F,...  112 us

profile of v5, /device:TPU:1, one launch (start us, length us, event | category | flops | bytes accessed | tf_op | source)
XLA Modules:
  0.0 113.3 jit_solution(6441800513896076213)
XLA Ops:
  0.6 111.7 %shard_map.119 = (bf16[32,4096]{1,0:T(8,128)(2,1)S(1)}, bf16[448,256]{1,0:T(8,128)(2,1)S(1)}, bf16[448,256]{1,0:T(8,128)(2,1)S(1)}, bf16[448,256]{1,0:T(8,128)(2,1)S(1)}, f32[1,4096]{1,0:T(1,128)S(1)}) custom-call(bf16[32,4096]{1,0:T(8,128)(2,1)} %inputs.1, bf16[448,512]{1,0:T(8,128)(2,1)} %bitcast.10, bf16[448,512]{1,0:T(8,128)(2,1)} %bitcast.11, ...), custom_call_target="tpu_custom_call" | custom-call | tf_op jit(solution)/shard_map/pallas_call | solution.py:597
  112.4 1.0 shard_map.120

commit v6 on v5

--- a/solution.py
+++ b/solution.py
@@ -20,52 +20,38 @@
 RW = (9, 10, 6, 7)
 ORDER = (
     ('G', 'e0', 0), ('G', 'e0', 3), ('G', 'e0', 1), ('G', 's2', 1, 0), ('G', 's2', 3, 0), ('prefac',), ('normed',),
-    ('G', 's2', 0, 0), ('G', 'e0', 2), ('G', 's2', 2, 0), ('nx',), ('N', 'e0', 2), ('G', 'f2', 1, 0, 3),
-    ('G', 'f2', 1, 0, 1), ('G', 'f1', 0, 3), ('G', 'f1', 0, 1), ('G', 's2', 0, 3), ('G', 's2', 0, 1),
-    ('G', 'f2', 3, 0, 3), ('G', 'f2', 3, 0, 1), ('hx',), ('G', 'f2', 0, 0, 3), ('G', 'f2', 0, 0, 1),
-    ('G', 'f1', 3, 3), ('G', 'f1', 3, 1), ('G', 'f2', 2, 0, 3), ('G', 'f2', 2, 0, 1), ('G', 's2', 3, 3),
-    ('N', 'f1', 2, 3), ('N', 'f1', 2, 1), ('G', 'f1', 1, 3), ('G', 'f1', 1, 1), ('G', 's2', 1, 3),
-    ('G', 'f2', 0, 3, 3), ('G', 'f2', 0, 3, 1), ('G', 'f2', 0, 1, 3), ('G', 'f2', 0, 1, 1), ('N', 'e0', 3),
-    ('G', 'f1', 2, 3), ('G', 'f1', 2, 1), ('G', 's2', 2, 3), ('G', 'e3', 0), ('G', 's2', 0, 2), ('G', 'e3', 3),
-    ('G', 'f2', 3, 3, 3), ('G', 'f2', 3, 3, 1), ('N', 'e3', 2), ('N', 'e0', 0), ('G', 'e3', 1), ('G', 's2', 2, 1),
-    ('G', 'f2', 1, 3, 3), ('G', 'f2', 1, 3, 1), ('G', 's2', 1, 1), ('N', 'e0', 1), ('N', 'f1', 3, 3),
-    ('N', 'f1', 3, 1), ('G', 's2', 1, 2), ('G', 'f2', 2, 3, 3), ('G', 'f2', 2, 3, 1), ('G', 'e3', 2),
-    ('G', 'f2', 0, 2, 3), ('G', 'f2', 0, 2, 1), ('G', 's2', 2, 2), ('N', 's2', 2, 0), ('N', 'f1', 0, 3),
-    ('N', 'f1', 0, 1), ('G', 'f2', 2, 1, 3), ('G', 'f2', 2, 1, 1), ('G', 's2', 3, 1), ('G', 'f2', 1, 1, 3),
-    ('G', 'f2', 1, 1, 1), ('N', 'f1', 1, 3), ('N', 'f1', 1, 1), ('G', 's2', 3, 2), ('G', 'f2', 1, 2, 3),
-    ('G', 'f2', 1, 2, 1), ('N', 'e3', 3), ('G', 'done', 0), ('gh', 0), ('N', 's2', 0, 0), ('N', 's2', 2, 3),
-    ('G', 'f2', 2, 2, 3), ('G', 'f2', 2, 2, 1), ('N', 'f2', 2, 0, 3), ('N', 'f2', 2, 0, 1), ('N', 's2', 0, 3),
-    ('dr', 0), ('D', 'part', 2), ('D', 'x2'), ('G', 'f2', 3, 1, 3), ('G', 'f2', 3, 1, 1), ('N', 'e3', 0),
-    ('N', 's2', 2, 1), ('N', 'e3', 1), ('N', 's2', 0, 1), ('G', 'f2', 3, 2, 3), ('G', 'f2', 3, 2, 1),
-    ('G', 'done', 1), ('gh', 1), ('N', 's2', 0, 2), ('N', 's2', 2, 2), ('N', 'f2', 2, 3, 3), ('N', 'f2', 2, 3, 1),
-    ('N', 'f2', 0, 0, 3), ('N', 'f2', 0, 0, 1), ('G', 'done', 2), ('gh', 2), ('N', 's2', 1, 0), ('dr', 1),
-    ('D', 'part', 1), ('N', 'f2', 0, 3, 3), ('N', 'f2', 0, 3, 1), ('D', 'x1'), ('dr', 2), ('D', 'part', 3),
-    ('N', 'f2', 2, 1, 3), ('N', 'f2', 2, 1, 1), ('D', 'x3'), ('N', 's2', 1, 3), ('G', 'done', 3), ('N', 's2', 1, 1),
-    ('N', 'f2', 0, 1, 3), ('N', 'f2', 0, 1, 1), ('gh', 3), ('acts',), ('N', 'f2', 0, 2, 3), ('N', 'f2', 0, 2, 1),
-    ('tr',), ('N', 'f2', 2, 2, 3), ('N', 'f2', 2, 2, 1), ('pp', 2), ('pp', 6), ('pp', 7), ('wready',),
-    ('R', 'r0', 3, 2), ('R', 'r0', 3, 1), ('pp', 1), ('N', 's2', 1, 2), ('R', 'r0', 3, 3), ('N', 's2', 3, 0),
-    ('N', 's2', 3, 3), ('pp', 4), ('N', 'f2', 1, 0, 3), ('N', 'f2', 1, 0, 1), ('N', 'f2', 1, 3, 3),
-    ('N', 'f2', 1, 3, 1), ('R', 'r0', 3, 0), ('dr', 3), ('D', 'part', 0), ('N', 'f2', 1, 1, 3), ('N', 'f2', 1, 1, 1),
-    ('pp', 3), ('N', 'done', 0), ('W', 'part', 2), ('W', 'x2'), ('N', 's2', 3, 1), ('N', 's2', 3, 2),
-    ('N', 'f2', 1, 2, 3), ('N', 'f2', 1, 2, 1), ('R', 'r1', 3, 2, 0), ('R', 'r1', 3, 2, 1), ('R', 'r1', 3, 1, 0),
-    ('R', 'r1', 3, 1, 1), ('R', 'r1', 3, 3, 0), ('R', 'r1', 3, 3, 1), ('D', 'cross'), ('R', 'r0', 1, 2),
-    ('R', 'r1', 3, 0, 0), ('R', 'r1', 3, 0, 1), ('pp', 0), ('R', 'r0', 0, 2), ('pp', 5), ('R', 'r0', 2, 2),
-    ('N', 'f2', 3, 0, 3), ('N', 'f2', 3, 0, 1), ('N', 'f2', 3, 3, 3), ('N', 'f2', 3, 3, 1), ('N', 'done', 2),
-    ('W', 'part', 3), ('R', 'r0', 2, 1), ('R', 'r0', 2, 3), ('R', 'r0', 2, 0), ('W', 'x3i'), ('N', 'f2', 3, 1, 3),
-    ('N', 'f2', 3, 1, 1), ('N', 'f2', 3, 2, 3), ('N', 'f2', 3, 2, 1), ('R', 'r2', 3, 2), ('N', 'done', 1),
-    ('W', 'part', 1), ('R', 'r1', 2, 2, 0), ('R', 'r1', 2, 2, 1), ('R', 'r1', 0, 2, 0), ('R', 'r1', 0, 2, 1),
-    ('R', 'r1', 1, 2, 0), ('R', 'r1', 1, 2, 1), ('W', 'x1i'), ('R', 'r2', 3, 1), ('R', 'r2', 3, 3),
-    ('R', 'r1', 2, 1, 0), ('R', 'r1', 2, 1, 1), ('R', 'r1', 2, 3, 0), ('R', 'r1', 2, 3, 1), ('R', 'r1', 2, 0, 0),
-    ('R', 'r1', 2, 0, 1), ('W', 'x3d'), ('W', 'x1d'), ('N', 'done', 3), ('W', 'part', 0), ('D', 'fin'),
-    ('R', 'r2', 2, 2), ('R', 'r0', 0, 1), ('gain0',), ('R', 'r2', 0, 2), ('R', 'r0', 0, 3), ('R', 'r4', 3, 0),
-    ('R', 'r4', 3, 1), ('R', 'r2', 3, 0), ('R', 'r2', 1, 2), ('R', 'r0', 0, 0), ('R', 'r2', 2, 1), ('R', 'r0', 1, 1),
-    ('R', 'r4', 2, 0), ('R', 'r2', 2, 3), ('R', 'r4', 2, 1), ('R', 'r0', 1, 3), ('R', 'r0', 1, 0), ('R', 'r2', 2, 0),
-    ('W', 'cross'), ('R', 'r1', 0, 1, 0), ('R', 'r1', 0, 1, 1), ('R', 'r1', 0, 3, 1), ('R', 'r1', 0, 3, 0),
-    ('R', 'r5', 3), ('R', 'r1', 0, 0, 1), ('R', 'r1', 0, 0, 0), ('R', 'r5', 2), ('R', 'r1', 1, 1, 1), ('gain1',),
-    ('R', 'r1', 1, 1, 0), ('R', 'r1', 1, 3, 0), ('R', 'r1', 1, 3, 1), ('R', 'r1', 1, 0, 1), ('R', 'r1', 1, 0, 0),
-    ('R', 'r2', 0, 1), ('R', 'r4', 0, 0), ('R', 'r2', 0, 3), ('R', 'r4', 0, 1), ('R', 'r2', 0, 0), ('R', 'r2', 1, 1),
-    ('R', 'r4', 1, 0), ('R', 'r2', 1, 3), ('R', 'r4', 1, 1), ('W', 'fin'), ('R', 'r2', 1, 0), ('gain2',),
-    ('R', 'r5', 0), ('R', 'r5', 1), ('fin',),
+    ('G', 's2', 0, 0), ('G', 'e0', 2), ('G', 's2', 2, 0), ('nx',), ('N', 'e0', 2), ('G', 'f2', 1, 0),
+    ('G', 'f1', 0, 3), ('G', 'f1', 0, 1), ('G', 's2', 0, 3), ('G', 's2', 0, 1), ('G', 'f2', 3, 0), ('hx',),
+    ('G', 'f2', 0, 0), ('G', 'f1', 3, 3), ('G', 'f1', 3, 1), ('G', 'f2', 2, 0), ('G', 's2', 3, 3), ('N', 'f1', 2, 3),
+    ('N', 'f1', 2, 1), ('G', 'f1', 1, 3), ('G', 'f1', 1, 1), ('G', 's2', 1, 3), ('G', 'f2', 0, 3), ('G', 'f2', 0, 1),
+    ('N', 'e0', 3), ('G', 'f1', 2, 3), ('G', 'f1', 2, 1), ('G', 's2', 2, 3), ('G', 'e3', 0), ('G', 's2', 0, 2),
+    ('G', 'e3', 3), ('G', 'f2', 3, 3), ('N', 'e3', 2), ('N', 'e0', 0), ('G', 'e3', 1), ('G', 's2', 2, 1),
+    ('G', 'f2', 1, 3), ('G', 's2', 1, 1), ('N', 'e0', 1), ('N', 'f1', 3, 3), ('N', 'f1', 3, 1), ('G', 's2', 1, 2),
+    ('G', 'f2', 2, 3), ('G', 'e3', 2), ('G', 'f2', 0, 2), ('G', 's2', 2, 2), ('N', 's2', 2, 0), ('N', 'f1', 0, 3),
+    ('N', 'f1', 0, 1), ('G', 'f2', 2, 1), ('G', 's2', 3, 1), ('G', 'f2', 1, 1), ('N', 'f1', 1, 3), ('N', 'f1', 1, 1),
+    ('G', 's2', 3, 2), ('G', 'f2', 1, 2), ('N', 'e3', 3), ('G', 'done', 0), ('gh', 0), ('N', 's2', 0, 0),
+    ('N', 's2', 2, 3), ('G', 'f2', 2, 2), ('N', 'f2', 2, 0), ('N', 's2', 0, 3), ('dr', 0), ('D', 'part', 2),
+    ('D', 'x2'), ('G', 'f2', 3, 1), ('N', 'e3', 0), ('N', 's2', 2, 1), ('N', 'e3', 1), ('N', 's2', 0, 1),
+    ('G', 'f2', 3, 2), ('G', 'done', 1), ('gh', 1), ('N', 's2', 0, 2), ('N', 's2', 2, 2), ('N', 'f2', 2, 3),
+    ('N', 'f2', 0, 0), ('G', 'done', 2), ('gh', 2), ('N', 's2', 1, 0), ('dr', 1), ('D', 'part', 1), ('N', 'f2', 0, 3),
+    ('D', 'x1'), ('dr', 2), ('D', 'part', 3), ('N', 'f2', 2, 1), ('D', 'x3'), ('N', 's2', 1, 3), ('G', 'done', 3),
+    ('N', 's2', 1, 1), ('N', 'f2', 0, 1), ('gh', 3), ('acts',), ('N', 'f2', 0, 2), ('tr',), ('N', 'f2', 2, 2),
+    ('pp', 2), ('pp', 6), ('pp', 7), ('wready',), ('R', 'r0', 3, 2), ('R', 'r0', 3, 1), ('pp', 1), ('N', 's2', 1, 2),
+    ('R', 'r0', 3, 3), ('N', 's2', 3, 0), ('N', 's2', 3, 3), ('pp', 4), ('N', 'f2', 1, 0), ('N', 'f2', 1, 3),
+    ('R', 'r0', 3, 0), ('dr', 3), ('D', 'part', 0), ('N', 'f2', 1, 1), ('pp', 3), ('N', 'done', 0), ('W', 'part', 2),
+    ('W', 'x2'), ('N', 's2', 3, 1), ('N', 's2', 3, 2), ('N', 'f2', 1, 2), ('R', 'r1', 3, 2), ('R', 'r1', 3, 1),
+    ('R', 'r1', 3, 3), ('D', 'cross'), ('R', 'r0', 1, 2), ('R', 'r1', 3, 0), ('pp', 0), ('R', 'r0', 0, 2), ('pp', 5),
+    ('R', 'r0', 2, 2), ('N', 'f2', 3, 0), ('N', 'f2', 3, 3), ('N', 'done', 2), ('W', 'part', 3), ('R', 'r0', 2, 1),
+    ('R', 'r0', 2, 3), ('R', 'r0', 2, 0), ('W', 'x3i'), ('N', 'f2', 3, 1), ('N', 'f2', 3, 2), ('R', 'r2', 3, 2),
+    ('N', 'done', 1), ('W', 'part', 1), ('R', 'r1', 2, 2), ('R', 'r1', 0, 2), ('R', 'r1', 1, 2), ('W', 'x1i'),
+    ('R', 'r2', 3, 1), ('R', 'r2', 3, 3), ('R', 'r1', 2, 1), ('R', 'r1', 2, 3), ('R', 'r1', 2, 0), ('W', 'x3d'),
+    ('W', 'x1d'), ('N', 'done', 3), ('W', 'part', 0), ('D', 'fin'), ('R', 'r2', 2, 2), ('R', 'r0', 0, 1), ('gain0',),
+    ('R', 'r2', 0, 2), ('R', 'r0', 0, 3), ('R', 'r4', 3), ('R', 'r2', 3, 0), ('R', 'r2', 1, 2), ('R', 'r0', 0, 0),
+    ('R', 'r2', 2, 1), ('R', 'r0', 1, 1), ('R', 'r2', 2, 3), ('R', 'r4', 2), ('R', 'r0', 1, 3), ('R', 'r0', 1, 0),
+    ('R', 'r2', 2, 0), ('W', 'cross'), ('R', 'r1', 0, 1), ('R', 'r1', 0, 3), ('R', 'r5', 3), ('R', 'r1', 0, 0),
+    ('R', 'r5', 2), ('gain1',), ('R', 'r1', 1, 1), ('R', 'r1', 1, 3), ('R', 'r1', 1, 0), ('R', 'r2', 0, 1),
+    ('R', 'r2', 0, 3), ('R', 'r4', 0), ('R', 'r2', 0, 0), ('R', 'r2', 1, 1), ('R', 'r2', 1, 3), ('R', 'r4', 1),
+    ('W', 'fin'), ('R', 'r2', 1, 0), ('gain2',), ('R', 'r5', 0), ('R', 'r5', 1), ('fin',),
 )
 RELS = (2, 1, 3, 0)
 
@@ -183,24 +169,25 @@
             i = KS.index(k)
             ref = self.piece(k, 0)
             src = ref if self.own is None or k else self.own
-            self.push(src, ref, 3 + 2 * i + 1, self.dev2(1))
-            self.push(src, ref, 3 + 2 * i, self.dev2(3))
+            self.push(src, ref, 3 + i, self.dev2(1))
+            self.push(src, ref, 3 + i, self.dev2(3))
 
         def f1(self, k):
             h = k // 2
             recv(self.piece(k, 0), self.r(h), self.s(h), self.dev1(k))
             self.push(self.half(k, 0, h), self.half(k, 0, h), 2, self.dev1(4 - k))
 
-        def f2(self, k, kk):
-            i, h = KS.index(k), kk // 2
-            recv(self.piece(k, kk), self.r(3 + 2 * i + h), self.sem, self.dev2(kk))
-            self.push(self.half(k, kk, h), self.half(k, kk, h), 11, self.dev2(4 - kk))
+        def f2(self, k):
+            i = KS.index(k)
+            recv(self.group_t(2), self.r(3 + i), self.sem, self.dev2(1))
+            self.push(self.half(k, 1, 0), self.half(k, 1, 0), 7, self.dev2(3))
+            self.push(self.half(k, 3, 1), self.half(k, 3, 1), 7, self.dev2(1))
 
         def e3(self):
             recv(self.piece(2, 0), self.r(2), self.sem, self.dev1(1))
 
         def done(self):
-            recv(self.group_t(4), self.r(11), self.sem, self.dev2(1))
+            recv(self.group_t(4), self.r(7), self.sem, self.dev2(1))
 
         def settle(self):
             wait_sent(self.group_t(15), self.sem, self.dev1(1))
@@ -266,7 +253,7 @@
             a1[rows, :] = up * (s * (1.0 + gp * (1.0 - s)))
             act_t[0, rows, :] = (gs * up).astype(BF)
 
-        sent.append(send(act_t.at[0], act_s.at[0], c_s.at[1], c_r.at[1], sib))
+        send(act_t.at[0], act_s.at[0], c_s.at[1], c_r.at[1], sib)
 
     begun = set()
 
@@ -281,7 +268,7 @@
             j = 2 * ring(x, RELS[q]) + i
             src = g_all.at[:, :, pl.ds(pl.multiple_of((2 * j + oc) * 256, 256), 256)]
             dst = g_sib.at[:, :, pl.ds(pl.multiple_of(j * 256, 256), 256)]
-            sent.append(send(src, dst, c_s.at[4 + 2 * q + i], c_r.at[4 + 2 * q + i], sib))
+            send(src, dst, c_s.at[2], c_r.at[3 + q], sib)
 
     def act_grads():
         @pl.loop(0, F // 64)
@@ -292,7 +279,7 @@
             act_t[2, rows, :] = (v * a2[rows, :]).astype(BF)
 
         for i in (1, 2):
-            sent.append(send(act_t.at[i], act_s.at[i], c_s.at[1 + i], c_r.at[1 + i], sib))
+            send(act_t.at[i], act_s.at[i], c_s.at[1], c_r.at[2], sib)
 
     def turn():
         @pl.loop(0, 4)
@@ -305,14 +292,11 @@
         recv(act_s.at[0], c_r.at[1], c_s.at[1], sib)
 
     def d_ready(q):
-        for i in range(2):
-            j = 2 * ring(x, RELS[q]) + i
-            dst = g_sib.at[:, :, pl.ds(pl.multiple_of(j * 256, 256), 256)]
-            recv(dst, c_r.at[4 + 2 * q + i], c_s.at[4 + 2 * q + i], sib)
+        dst = g_sib.at[:, :, pl.ds(pl.multiple_of(ring(x, RELS[q]) * 512, 512), 512)]
+        recv(dst, c_r.at[3 + q], c_s.at[2], sib)
 
     def w_ready():
-        for i in (1, 2):
-            recv(act_s.at[i], c_r.at[1 + i], c_s.at[1 + i], sib)
+        recv(act_s.at[pl.ds(1, 2)], c_r.at[2], c_s.at[1], sib)
 
     def add_rows(dst, srcs, rows, step):
         @pl.loop(0, rows // step)
@@ -501,39 +485,40 @@
 
         def r0(self, k):
             i = KS.index(k)
-            self.push(self.hblk(2, k, 0), rh.at[i, 0, :, self.cols], 2 * i, self.dev1(1))
-            self.push(self.hblk(2, k, 1), rh.at[i, 1, :, self.cols], 2 * i + 1, self.dev1(3))
-
-        def r1(self, k, h):
-            i, k1 = KS.index(k), 1 + 2 * h
-            src = rh.at[i, h, :, self.cols]
-            recv(src, self.r(2 * i + h), self.s(2 * i + h), self.dev1(4 - k1))
-            dst = self.hblk(k1, k, h)
-            dst[...] = (dst[...].astype(F32) + src[...].astype(F32)).astype(BF)
-            self.push(self.blk(k1, k), rf.at[i, h, :, self.cols], 8 + i, self.dev1(k1))
+            self.push(self.hblk(2, k, 0), rh.at[i, 0, :, self.cols], i, self.dev1(1))
+            self.push(self.hblk(2, k, 1), rh.at[i, 1, :, self.cols], i, self.dev1(3))
+
+        def r1(self, k):
+            i = KS.index(k)
+            recv(rh.at[i, :, :, self.cols], self.r(i), self.sem, self.dev1(1))
+            for h, k1 in ((0, 1), (1, 3)):
+                src = rh.at[i, h, :, self.cols]
+                dst = self.hblk(k1, k, h)
+                dst[...] = (dst[...].astype(F32) + src[...].astype(F32)).astype(BF)
+                self.push(self.blk(k1, k), rf.at[i, h, :, self.cols], 4 + i, self.dev1(k1))
 
         def r2(self, k):
             i = KS.index(k)
-            recv(rf.at[i, :, :, self.cols], self.r(8 + i), self.sem, self.dev1(1))
+            recv(rf.at[i, :, :, self.cols], self.r(4 + i), self.sem, self.dev1(1))
             v = self.blk(0, k)[...].astype(F32) + rf[i, 0, :, self.cols].astype(F32)
             v = v + rf[i, 1, :, self.cols].astype(F32)
             rs[i, :, self.cols] = v.astype(BF)
             if k == 2:
                 for h, k2 in ((0, 1), (1, 3)):
                     src = rs.at[i, pl.ds(16 * h, 16), self.cols]
-                    self.push(src, zh_buf.at[h, :, self.cols], 12 + h, self.dev2(k2))
-
-        def r4(self, h):
-            k2 = 1 + 2 * h
-            src = zh_buf.at[h, :, self.cols]
-            recv(src, self.r(12 + h), self.sem, self.dev2(4 - k2))
-            i = KS.index(k2)
-            dst = rs.at[i, pl.ds(16 * h, 16), self.cols]
-            dst[...] = (dst[...].astype(F32) + src[...].astype(F32)).astype(BF)
-            self.push(rs.at[i, :, self.cols], zf_buf.at[h, :, self.cols], 14, self.dev2(k2))
+                    self.push(src, zh_buf.at[h, :, self.cols], 8, self.dev2(k2))
+
+        def r4(self):
+            recv(zh_buf.at[:, :, self.cols], self.r(8), self.sem, self.dev2(1))
+            for h, k2 in ((0, 1), (1, 3)):
+                src = zh_buf.at[h, :, self.cols]
+                i = KS.index(k2)
+                dst = rs.at[i, pl.ds(16 * h, 16), self.cols]
+                dst[...] = (dst[...].astype(F32) + src[...].astype(F32)).astype(BF)
+                self.push(rs.at[i, :, self.cols], zf_buf.at[h, :, self.cols], 9, self.dev2(k2))
 
         def r5(self):
-            recv(zf_buf.at[:, :, self.cols], self.r(14), self.sem, self.dev2(1))
+            recv(zf_buf.at[:, :, self.cols], self.r(9), self.sem, self.dev2(1))
             v = rs[0, :, self.cols].astype(F32) + zf_buf[0, :, self.cols].astype(F32)
             gn[:, self.cols] = v + zf_buf[1, :, self.cols].astype(F32)
 
@@ -577,6 +562,8 @@
         RA[q].settle()
     wait_sent(gt.at[pl.ds(0, 15)], g_s.at[0], tdev(1))
     wait_sent(og.at[pl.ds(0, 15)], g_s.at[1], pdev(1))
+    wait_sent(act_t, c_s.at[1], sib)
+    wait_sent(g_sib, c_s.at[2], sib)
     for cp in sent:
         cp.wait_send()
 
@@ -616,8 +603,8 @@
             V((4, 2, F, 256), BF), V((2, F, 256), BF), V((2, 2, F, 256), BF), V((F, 256), BF),
             V((4, 2, 2, F, 256), BF), V((2, 2, F, 256), BF), V((2, 2, 2, F, 256), BF), V((2, F, 256), BF),
             V((16, 8, 256), F32), V((16, 8, 256), F32),
-            DMA((8,)), DMA((2, NQ)), DMA((2, NQ, 12)), DMA((NQ,)), DMA((NQ, 15)),
-            DMA((16,)), DMA((16,)), DMA((12,)), DMA((12,)), DMA((2,)), DMA((2,)),
+            DMA((8,)), DMA((2, NQ)), DMA((2, NQ, 8)), DMA((NQ,)), DMA((NQ, 10)),
+            DMA((16,)), DMA((16,)), DMA((3,)), DMA((7,)), DMA((2,)), DMA((2,)),
         ],
         compiler_params=pltpu.CompilerParams(
             collective_id=0, has_side_effects=True, vmem_limit_bytes=56 * 2**20

time: 113 us -> 113 us (level)
  no operation moved by 1% of the time
where the time goes in v6:
time: 113 us
  Pallas kernels  112 us (99%)
    pallas_call x1, Pallas kernels, body(): pl.pallas_call(kernel, out_shape=(V((32, D), BF), V((F, 256), BF), V((F,...  111 us

profile of v6, /device:TPU:1, one launch (start us, length us, event | category | flops | bytes accessed | tf_op | source)
XLA Modules:
  0.0 112.7 jit_solution(3688722157379993577)
XLA Ops:
  0.6 111.1 %shard_map.119 = (bf16[32,4096]{1,0:T(8,128)(2,1)S(1)}, bf16[448,256]{1,0:T(8,128)(2,1)S(1)}, bf16[448,256]{1,0:T(8,128)(2,1)S(1)}, bf16[448,256]{1,0:T(8,128)(2,1)S(1)}, f32[1,4096]{1,0:T(1,128)S(1)}) custom-call(bf16[32,4096]{1,0:T(8,128)(2,1)} %inputs.1, bf16[448,512]{1,0:T(8,128)(2,1)} %bitcast.10, bf16[448,512]{1,0:T(8,128)(2,1)} %bitcast.11, ...), custom_call_target="tpu_custom_call" | custom-call | tf_op jit(solution)/shard_map/pallas_call | solution.py:584
  111.7 1.0 shard_map.120
